TPU v7x, 32 devices: a whole 2x2x4 slice. The times are simulated.
32 devices in a mesh: section: 2 (over core), dp: 16 (over z, y, x).
Axes of the slice: x: 2, y: 2, z: 4, core: 2. Of those that a mesh axis runs over, the one named last changes fastest.
Arguments:
- tokens: bfloat16 [65536, 512], P('dp'), may hold values from -6 to 6
- lengths: int32 [32, 3], P('dp'), may hold values from 1 to 32, 64 in all within a row
- w_qkv: bfloat16 [512, 1536], replicated, may hold values from -0.25 to 0.25
- w_out: bfloat16 [512, 512], replicated, may hold values from -0.75 to 0.75
- w_sort: bfloat16 [512, 256], replicated, may hold values from -2.5 to 2.5
- gain_attn: float32 [512], replicated, may hold values from 0.5 to 1.5
- bias_attn: float32 [512], replicated, may hold values from -1.5 to 1.5
- gain_ffn: float32 [512], replicated, may hold values from 0.5 to 1.5
- bias_ffn: float32 [512], replicated, may hold values from -1.5 to 1.5
- w_up: bfloat16 [512, 2048], replicated, may hold values from -0.25 to 0.25
- bias_up: float32 [2048], replicated, may hold values from -1.5 to 1.5
- w_down: bfloat16 [2048, 512], replicated, may hold values from -0.125 to 0.125
- bias_down: float32 [512], replicated, may hold values from -1.5 to 1.5
- cotangent: bfloat16 [65536, 512], P('dp'), may hold values from -6 to 6
Outputs:
- ends: float32 [2, 65536, 512], P('section', 'dp')
- grad_qkv: float32 [512, 1536], replicated
- grad_out: float32 [512, 512], replicated
- grad_sort: float32 [512, 256], replicated
- grad_gain_attn: float32 [512], replicated
- grad_bias_attn: float32 [512], replicated
- grad_gain_ffn: float32 [512], replicated
- grad_bias_ffn: float32 [512], replicated
- grad_up: float32 [512, 2048], replicated
- grad_bias_up: float32 [2048], replicated
- grad_down: float32 [2048, 512], replicated
- grad_bias_down: float32 [512], replicated
Inputs may be any that keep to these rules, and one draw needn't show every extreme that they name: lengths in blocks of 32 tokens; each row sums to 64, and its longest sequence has exactly 32 blocks.
All inputs are finite; a program needn't handle non-finite values.
Results may differ from a plain program's by a relative error of at most 0.017.
Values may be sent and summed in bfloat16 or wider, within the bound.
A program may use at most 256 MiB of HBM per device.

v0:
```python
import math

import jax
import jax.numpy as jnp
from jax import lax
from jax.sharding import PartitionSpec as P

D = 512
HEADS = 8
HDIM = 64
BLK = 32
SINK = 8
SPAN = 32


highest = lax.Precision.HIGHEST


def shifted(value, axis, steps):
    count = lax.axis_size(axis)
    leading, last = (max(0, -steps), min(count, count - steps))
    return lax.ppermute(value, axis, [(source, source + steps) for source in range(leading, last)])


def layer_norm(features, norm_gain, norm_shift):
    average = jnp.mean(features, axis=-1, keepdims=True)
    centered = features - average
    variance = jnp.mean(centered * centered, axis=-1, keepdims=True)
    return centered * lax.rsqrt(variance + 1e-05) * norm_gain + norm_shift


def block_layout(seq_lengths, block_count):
    seq_ends = jnp.cumsum(seq_lengths, dtype=jnp.int32)
    places = jnp.arange(block_count, dtype=jnp.int32)
    passed = places[:, None] >= seq_ends[None, :]
    owners = jnp.sum(passed.astype(jnp.int32), axis=1, dtype=jnp.int32)
    first_block = jnp.sum(jnp.where(passed, seq_lengths[None, :], 0), axis=1, dtype=jnp.int32)
    same_seq = owners[:, None] == owners[None, :]
    eligible_pattern = same_seq & (places[None, :] <= places[:, None])
    earlier_quantity = same_seq & (places[None, :] < places[:, None])
    offset = places[None, :] - first_block[:, None]
    columns = jnp.arange(SPAN, dtype=jnp.int32)
    onehot_lines = (offset[:, :, None] == columns[None, None, :]).astype(jnp.float32)
    opening = places == first_block
    return (eligible_pattern, earlier_quantity, onehot_lines, opening)


def attend_mask(opening):
    positions = jnp.arange(BLK, dtype=jnp.int32)
    causal = positions[None, :] <= positions[:, None]
    block_count = opening.shape[0]
    near_ok = jnp.broadcast_to(causal[None], (block_count, BLK, BLK))
    far_ok = jnp.broadcast_to(jnp.logical_not(opening)[:, None, None], (block_count, BLK, BLK))
    return jnp.concatenate([near_ok, far_ok], axis=2)[:, None]


def doubly_stochastic_balance(
    permutation_score_table, onehot_lines, eligible_pattern, earlier_quantity
):
    placed = jnp.einsum("ihc,ijc->hij", permutation_score_table, onehot_lines, precision=highest)
    current = jnp.where(eligible_pattern[None], placed, -10000.0)
    for sweep in range(SINK):
        current = current - jax.nn.logsumexp(current, axis=2, keepdims=True)
        current = current - jax.nn.logsumexp(current, axis=1, keepdims=True)
    return jnp.where(earlier_quantity[None], jnp.exp(current), 0.0)


def attention_parts(rows_in, seq_lengths, w_qkv, w_out, w_sort, gain_attn, bias_attn):
    row_count = rows_in.shape[0]
    block_count = row_count // BLK
    layout = block_layout(seq_lengths, block_count)
    eligible_pattern, earlier_quantity, onehot_lines, opening = layout
    inputs = rows_in.astype(jnp.float32)
    normed = layer_norm(inputs, gain_attn, bias_attn)
    normed_low = normed.astype(jnp.bfloat16)
    packed = jnp.dot(normed_low, w_qkv, preferred_element_type=jnp.float32).astype(jnp.bfloat16)
    queries = packed[:, :D].reshape(block_count, BLK, HEADS, HDIM)
    keys_near = packed[:, D : 2 * D].reshape(block_count, BLK, HEADS, HDIM)
    values_near = packed[:, 2 * D :].reshape(block_count, BLK, HEADS, HDIM)
    summary = jnp.mean(normed.reshape(block_count, BLK, D), axis=1).astype(jnp.bfloat16)
    segment_scores_raw = jnp.dot(summary, w_sort, preferred_element_type=jnp.float32).reshape(
        block_count, HEADS, SPAN
    )
    segment_blend = doubly_stochastic_balance(
        segment_scores_raw, onehot_lines, eligible_pattern, earlier_quantity
    ).astype(jnp.bfloat16)
    keys_far = jnp.einsum(
        "hij,jthd->ithd", segment_blend, keys_near, preferred_element_type=jnp.float32
    ).astype(jnp.bfloat16)
    values_far = jnp.einsum(
        "hij,jthd->ithd", segment_blend, values_near, preferred_element_type=jnp.float32
    ).astype(jnp.bfloat16)
    keys_all = jnp.concatenate([keys_near, keys_far], axis=1)
    values_all = jnp.concatenate([values_near, values_far], axis=1)
    score_scale = 1.0 / math.sqrt(HDIM)
    scores = (
        jnp.einsum("ithd,ishd->ihts", queries, keys_all, preferred_element_type=jnp.float32)
        * score_scale
    )
    scores = jnp.where(attend_mask(opening), scores, -1000000000.0)
    softmax_out = jax.nn.softmax(scores, axis=-1)
    soft_low = softmax_out.astype(jnp.bfloat16)
    attended = jnp.einsum(
        "ihts,ishd->ithd", soft_low, values_all, preferred_element_type=jnp.float32
    )
    attended = attended.reshape(row_count, D).astype(jnp.bfloat16)
    middle = inputs + jnp.dot(attended, w_out, preferred_element_type=jnp.float32)
    return (
        middle,
        inputs,
        normed_low,
        queries,
        keys_near,
        values_near,
        summary,
        segment_scores_raw,
        segment_blend,
        keys_all,
        values_all,
        softmax_out,
        soft_low,
        attended,
        layout,
    )


def attention_back(rows_in, seq_lengths, grad_middle, w_qkv, w_out, w_sort, gain_attn, bias_attn):
    (
        middle,
        inputs,
        normed_low,
        queries,
        keys_near,
        values_near,
        summary,
        segment_scores_raw,
        segment_blend,
        keys_all,
        values_all,
        softmax_out,
        soft_low,
        attended,
        layout,
    ) = attention_parts(rows_in, seq_lengths, w_qkv, w_out, w_sort, gain_attn, bias_attn)
    eligible_pattern, earlier_quantity, onehot_lines, opening = layout
    row_count = rows_in.shape[0]
    block_count = row_count // BLK
    score_scale = 1.0 / math.sqrt(HDIM)
    grad_out = jnp.dot(attended.T, grad_middle, preferred_element_type=jnp.float32)
    grad_attended = jnp.dot(grad_middle, w_out.T, preferred_element_type=jnp.float32).astype(
        jnp.bfloat16
    )
    grad_attended = grad_attended.reshape(block_count, BLK, HEADS, HDIM)
    grad_soft = jnp.einsum(
        "ithd,ishd->ihts", grad_attended, values_all, preferred_element_type=jnp.float32
    )
    grad_values_all = jnp.einsum(
        "ihts,ithd->ishd", soft_low, grad_attended, preferred_element_type=jnp.float32
    )
    grad_scores = softmax_out * (
        grad_soft - jnp.sum(grad_soft * softmax_out, axis=-1, keepdims=True)
    )
    grad_scores = grad_scores.astype(jnp.bfloat16)
    grad_queries = (
        jnp.einsum("ihts,ishd->ithd", grad_scores, keys_all, preferred_element_type=jnp.float32)
        * score_scale
    ).astype(jnp.bfloat16)
    grad_keys_all = (
        jnp.einsum("ihts,ithd->ishd", grad_scores, queries, preferred_element_type=jnp.float32)
        * score_scale
    )
    grad_keys_far = grad_keys_all[:, BLK:].astype(jnp.bfloat16)
    grad_values_far = grad_values_all[:, BLK:].astype(jnp.bfloat16)
    grad_mixing = jnp.einsum(
        "ithd,jthd->hij", grad_keys_far, keys_near, preferred_element_type=jnp.float32
    )
    grad_mixing = grad_mixing + jnp.einsum(
        "ithd,jthd->hij", grad_values_far, values_near, preferred_element_type=jnp.float32
    )
    grad_keys = grad_keys_all[:, :BLK] + jnp.einsum(
        "hij,ithd->jthd", segment_blend, grad_keys_far, preferred_element_type=jnp.float32
    )
    grad_values = grad_values_all[:, :BLK] + jnp.einsum(
        "hij,ithd->jthd", segment_blend, grad_values_far, preferred_element_type=jnp.float32
    )
    grad_keys = grad_keys.astype(jnp.bfloat16)
    grad_values = grad_values.astype(jnp.bfloat16)

    def sort_table(permutation_score_table):
        return doubly_stochastic_balance(
            permutation_score_table, onehot_lines, eligible_pattern, earlier_quantity
        )

    ignored, sort_pull = jax.vjp(sort_table, segment_scores_raw)
    grad_logits = sort_pull(grad_mixing)[0].astype(jnp.bfloat16).reshape(block_count, HEADS * SPAN)
    grad_sort = jnp.dot(summary.T, grad_logits, preferred_element_type=jnp.float32)
    grad_summary = jnp.dot(grad_logits, w_sort.T, preferred_element_type=jnp.float32)
    grad_packed = jnp.concatenate(
        [
            grad_queries.reshape(row_count, D),
            grad_keys.reshape(row_count, D),
            grad_values.reshape(row_count, D),
        ],
        axis=1,
    )
    grad_qkv = jnp.dot(normed_low.T, grad_packed, preferred_element_type=jnp.float32)
    grad_normed = jnp.dot(grad_packed, w_qkv.T, preferred_element_type=jnp.float32)
    grad_normed = grad_normed + jnp.repeat(grad_summary / BLK, BLK, axis=0)
    unused, norm_pull = jax.vjp(layer_norm, inputs, gain_attn, bias_attn)
    grad_inputs, grad_gain, grad_bias = norm_pull(grad_normed)
    grad_inputs = grad_inputs + grad_middle.astype(jnp.float32)
    return (grad_inputs, (grad_qkv, grad_out, grad_sort, grad_gain, grad_bias))


def ffn_back(middle_low, cot_rows, gain_ffn, bias_ffn, w_up, bias_up, w_down, bias_down):
    middle = middle_low.astype(jnp.float32)
    normed = layer_norm(middle, gain_ffn, bias_ffn)
    normed_low = normed.astype(jnp.bfloat16)
    hidden_pre = jnp.dot(normed_low, w_up, preferred_element_type=jnp.float32) + bias_up
    active_low = jax.nn.gelu(hidden_pre).astype(jnp.bfloat16)
    outputs = middle + jnp.dot(active_low, w_down, preferred_element_type=jnp.float32) + bias_down
    grad_down = jnp.dot(active_low.T, cot_rows, preferred_element_type=jnp.float32)
    grad_bias_down = jnp.sum(cot_rows, axis=0, dtype=jnp.float32)
    grad_active = jnp.dot(cot_rows, w_down.T, preferred_element_type=jnp.float32)
    unused, gelu_pull = jax.vjp(jax.nn.gelu, hidden_pre)
    grad_pre = gelu_pull(grad_active)[0].astype(jnp.bfloat16)
    grad_bias_up = jnp.sum(grad_pre, axis=0, dtype=jnp.float32)
    grad_up = jnp.dot(normed_low.T, grad_pre, preferred_element_type=jnp.float32)
    grad_normed = jnp.dot(grad_pre, w_up.T, preferred_element_type=jnp.float32)
    ignored, norm_pull = jax.vjp(layer_norm, middle, gain_ffn, bias_ffn)
    grad_mid, grad_gain, grad_bias = norm_pull(grad_normed)
    grad_mid = (grad_mid + cot_rows.astype(jnp.float32)).astype(jnp.bfloat16)
    return (
        outputs,
        grad_mid,
        (grad_gain, grad_bias, grad_up, grad_bias_up, grad_down, grad_bias_down),
    )


def spread_out(flat, templates):
    pieces = []
    offset = 0
    for member in templates:
        pieces.append(flat[offset : offset + member.size].reshape(member.shape))
        offset = offset + member.size
    return tuple(pieces)


def shards(
    tokens,
    lengths,
    w_qkv,
    w_out,
    w_sort,
    gain_attn,
    bias_attn,
    gain_ffn,
    bias_ffn,
    w_up,
    bias_up,
    w_down,
    bias_down,
    cotangent,
):
    micro_count = lengths.shape[0]
    row_count = tokens.shape[0] // micro_count
    first_section = lax.axis_index("section") == 0
    attn_weights = (w_qkv, w_out, w_sort, gain_attn, bias_attn)
    ffn_weights = (gain_ffn, bias_ffn, w_up, bias_up, w_down, bias_down)

    def produce(rows_in, seq_lengths):
        return attention_parts(rows_in, seq_lengths, *attn_weights)[0].astype(jnp.bfloat16)

    def blank_produce(rows_in, seq_lengths):
        return jnp.zeros((rows_in.shape[0], D), jnp.bfloat16)

    def consume(middle_low, cot_rows):
        return ffn_back(middle_low, cot_rows, *ffn_weights)

    def blank_consume(middle_low, cot_rows):
        rows = middle_low.shape[0]
        return (
            jnp.zeros((rows, D), jnp.float32),
            jnp.zeros((rows, D), jnp.bfloat16),
            tuple((jnp.zeros(member.shape, jnp.float32) for member in ffn_weights)),
        )

    def absorb(rows_in, seq_lengths, grad_middle):
        return attention_back(rows_in, seq_lengths, grad_middle, *attn_weights)

    def blank_absorb(rows_in, seq_lengths, grad_middle):
        rows = rows_in.shape[0]
        return (
            jnp.zeros((rows, D), jnp.float32),
            tuple((jnp.zeros(member.shape, jnp.float32) for member in attn_weights)),
        )

    attn_sums = tuple((jnp.zeros(member.shape, jnp.float32) for member in attn_weights))
    ffn_sums = tuple((jnp.zeros(member.shape, jnp.float32) for member in ffn_weights))
    arrived = []
    for micro_index in range(micro_count):
        rows_in = tokens[micro_index * row_count : (micro_index + 1) * row_count]
        outgoing = lax.cond(first_section, produce, blank_produce, rows_in, lengths[micro_index])
        arrived.append(shifted(outgoing, "section", 1))
    results = [None] * micro_count
    grads_in = [None] * micro_count
    for micro_index in reversed(range(micro_count)):
        rows_in = tokens[micro_index * row_count : (micro_index + 1) * row_count]
        cot_rows = cotangent[micro_index * row_count : (micro_index + 1) * row_count]
        outputs, grad_middle, ffn_part = lax.cond(
            first_section, blank_consume, consume, arrived[micro_index], cot_rows
        )
        returned = shifted(grad_middle, "section", -1)
        grad_inputs, attn_part = lax.cond(
            first_section, absorb, blank_absorb, rows_in, lengths[micro_index], returned
        )
        results[micro_index] = outputs
        grads_in[micro_index] = grad_inputs
        attn_sums = jax.tree.map(jnp.add, attn_sums, attn_part)
        ffn_sums = jax.tree.map(jnp.add, ffn_sums, ffn_part)
    grad_rows = jnp.concatenate(grads_in, axis=0)
    out_rows = jnp.concatenate(results, axis=0)
    ends = jnp.where(first_section, grad_rows, out_rows)[None]
    attn_flat = jnp.concatenate([member.reshape(-1) for member in attn_sums])
    ffn_flat = jnp.concatenate([member.reshape(-1) for member in ffn_sums])
    flat_width = max(attn_flat.shape[0], ffn_flat.shape[0])
    attn_padded = jnp.pad(attn_flat, (0, flat_width - attn_flat.shape[0]))
    keep_flat = jnp.where(first_section, attn_padded, ffn_flat)
    zero_flat = jnp.zeros_like(keep_flat)
    attn_own = jnp.where(first_section, keep_flat, zero_flat)
    ffn_own = jnp.where(first_section, zero_flat, keep_flat)
    pieces = spread_out(attn_own, attn_sums) + spread_out(ffn_own, ffn_sums)
    totals = lax.psum(
        (
            pieces[0],
            pieces[1],
            pieces[2],
            pieces[3],
            pieces[4],
            pieces[5],
            pieces[6],
            pieces[7],
            pieces[8],
            pieces[9],
            pieces[10],
        ),
        ("section", "dp"),
    )
    return (
        ends,
        totals[0],
        totals[1],
        totals[2],
        totals[3],
        totals[4],
        totals[5],
        totals[6],
        totals[7],
        totals[8],
        totals[9],
        totals[10],
    )


def solution(mesh):
    return jax.shard_map(
        shards,
        mesh=mesh,
        in_specs=(
            P("dp", None),
            P("dp", None),
            P(),
            P(),
            P(),
            P(),
            P(),
            P(),
            P(),
            P(),
            P(),
            P(),
            P(),
            P("dp", None),
        ),
        out_specs=(P("section", "dp", None), P(), P(), P(), P(), P(), P(), P(), P(), P(), P(), P()),
        check_vma=False,
    )
```

profile of v0, /device:TPU:0, one launch (start us, length us, event | category | flops | bytes accessed | tf_op | source)
XLA Modules:
  0.0 1560.4 jit_solution(648108415734186109)
XLA Ops:
  11.9 164.8 %conditional.9 = (bf16[2048,512]{1,0:T(8,128)(2,1)}) conditional(s32[]{:T(128)} %convert_element_type.284, () %tuple.70, (bf16[2048,512]{1,0:T(8,128)(2,1)}, f32[512]{0:T(512)}, f32[512]{0:T(512)}, bf16[512,1536]{1,0:T(8,128)(2,1)}, s32[3]{0:T(128)S(1)}, /*index=5*/s32[1,3]{1,0:T(1,128)S(1)}, bf16[512,256]{1,0:T(8,128)(2,1)S(1)}, ...), branch_computations={%region_115.116_spmd, %region_116.157_spmd} | conditional | flops 4906217472 | bytes 153832928 | solution.py:303
  73.9 13.2 copy.1586
  87.0 12.5 fusion.240
  99.5 11.6 fusion.497
  138.8 13.1 copy.1587
  179.3 159.5 %conditional.6 = (bf16[2048,512]{1,0:T(8,128)(2,1)}) conditional(s32[]{:T(128)} %convert_element_type.284, () %tuple.64, (bf16[2048,512]{1,0:T(8,128)(2,1)S(1)}, f32[512]{0:T(512)}, f32[512]{0:T(512)}, bf16[512,1536]{1,0:T(8,128)(2,1)}, s32[3]{0:T(128)S(1)}, /*index=5*/s32[1,3]{1,0:T(1,128)S(1)}, bf16[512,256]{1,0:T(8,128)(2,1)S(1)}, ...), branch_computations={%region_0.0_spmd, %region_1.42_spmd} | conditional | flops 4906217472 | bytes 145444288 | solution.py:303
  236.8 13.2 copy.1405
  250.0 12.5 fusion.9
  262.5 11.6 fusion.492
  301.5 13.1 copy.1406
  340.3 15.1 conditional.10
  389.8 439.0 %conditional.11 = (f32[512,1536]{1,0:T(8,128)}, f32[512,512]{1,0:T(8,128)S(1)}, f32[512,256]{1,0:T(8,128)S(1)}, f32[512]{0:T(512)S(1)}, f32[512]{0:T(512)S(1)}, /*index=5*/f32[1,2048,512]{2,1,0:T(8,128)}) conditional(s32[]{:T(128)} %convert_element_type.284, () %tuple.69, (bf16[2048,512]{1,0:T(8,128)(2,1)}, f32[512]{0:T(512)}, f32[512]{0:T(512)}, ...), branch_computations={%region_167.168_spmd, %region_168.230_spmd} | conditional | flops 13603838976 | bytes 484496000 | solution.py:314
  478.2 13.1 copy.1640
  519.0 13.2 copy.1641
  532.2 12.5 fusion.325
  544.7 11.6 fusion.499
  580.7 11.4 multiply_reduce_fusion.1
  619.6 13.5 convolution_bitcast_fusion.1
  659.0 10.0 fusion.296
  687.3 10.3 multiply_bitcast_fusion.1
  776.9 10.0 fusion.297
  830.0 424.2 %conditional.8 = (f32[512,1536]{1,0:T(8,128)}, f32[512,512]{1,0:T(8,128)}, f32[512,256]{1,0:T(8,128)S(1)}, f32[512]{0:T(512)S(1)}, f32[512]{0:T(512)S(1)}, /*index=5*/f32[1,2048,512]{2,1,0:T(8,128)}) conditional(s32[]{:T(128)} %convert_element_type.284, () %tuple.63, (bf16[2048,512]{1,0:T(8,128)(2,1)S(1)}, f32[512]{0:T(512)}, f32[512]{0:T(512)}, ...), branch_computations={%region_52.53_spmd, %region_53.115_spmd} | conditional | flops 13603838976 | bytes 497013312 | solution.py:314
  919.5 13.1 copy.1459
  957.4 13.4 copy.1460
  970.7 12.5 fusion.94
  983.2 11.6 fusion.494
  1020.4 10.1 multiply_reduce_fusion
  1058.0 13.3 convolution_bitcast_fusion
  1121.2 10.3 multiply_bitcast_fusion
  1299.4 43.9 %all-reduce.1 = (f32[512]{0:T(512)}, f32[512]{0:T(512)}, f32[512]{0:T(512)}, f32[512]{0:T(512)}, f32[2048]{0:T(1024)}, /*index=5*/f32[512]{0:T(512)}) all-reduce(f32[512]{0:T(512)S(1)} %get-tuple-element.460, f32[512]{0:T(512)S(1)} %get-tuple-element.461, ...), channel_id=1, replica_groups=mesh['section'=2,'dp'=16] {'section','dp'}, use_global_device_ids=true, to_apply=%region_233.234 | all-reduce | flops 4608 | bytes 36864 | tf_op jit(solution)/shard_map/psum | solution.py:333
  1343.4 10.3 maximum_select_fusion
  1353.7 188.2 %all-reduce.5.cloned.1.call-done = (f32[512,1536]{1,0:T(8,128)}, f32[512,512]{1,0:T(8,128)}, f32[512,256]{1,0:T(8,128)}, f32[512,2048]{1,0:T(8,128)}, f32[2048,512]{1,0:T(8,128)}) async-done(((f32[512,1536]{1,0:T(8,128)}, f32[512,512]{1,0:T(8,128)}, f32[512,256]{1,0:T(8,128)}, f32[512,2048]{1,0:T(8,128)}, f32[2048,512]{1,0:T(8,128)}), (f32[512,1536]{1,0:T(8,128)}, f32[512,512]{1,0:T(8,128)}, ...) | async-done | bytes 13107216 | tf_op jit(solution)/shard_map/psum | solution.py:333
  (1307 shorter events, 997.7 us)
Async XLA Ops:
  7.2 1534.7 %all-reduce.5.cloned.1.call-start = ((), (), s32[]{:S(2)}) async-start(), calls=%async_computation | async-start | bytes 26214400 | tf_op jit(solution)/shard_map/psum | solution.py:333
  8.0 171.3 %copy-start.235 = (s32[1,3]{1,0:T(1,128)}, s32[1,3]{1,0:T(1,128)S(1)}, u32[]{:S(2)}) copy-start(s32[1,3]{1,0:T(1,128)S(1)} %get-tuple-element.456) | copy-start | bytes 40
  8.0 171.3 %copy-start.238 = (s32[3]{0:T(128)}, s32[3]{0:T(128)S(1)}, u32[]{:S(2)}) copy-start(s32[3]{0:T(128)S(1)} %get-tuple-element.457) | copy-start | bytes 40
  11.9 167.4 %copy-start = (bf16[2048,512]{1,0:T(8,128)(2,1)}, bf16[2048,512]{1,0:T(8,128)(2,1)S(1)}, u32[]{:S(2)}) copy-start(bf16[2048,512]{1,0:T(8,128)(2,1)S(1)} %get-tuple-element.454) | copy-start | bytes 6291460
  176.7 163.6 %collective-permute-start.2 = (bf16[2048,512]{1,0:T(8,128)(2,1)}, bf16[2048,512]{1,0:T(8,128)(2,1)}, u32[]{:S(2)}, u32[]{:S(2)}) collective-permute-start(bf16[2048,512]{1,0:T(8,128)(2,1)} %get-tuple-element.536), channel_id=1, source_target_pairs={{0,16},{1,17},{2,18},{3,19},{4,20},{5,21},{6,22},{7,23},{8,24},{9,... | collective-permute-start | bytes 6291464 | tf_op jit(solution)/shard_map/ppermute | solution.py:22
  179.3 161.0 %copy-start.222 = (f32[512]{0:T(512)S(1)}, f32[512]{0:T(512)}, u32[]{:S(2)}) copy-start(f32[512]{0:T(512)} %param.33) | copy-start | bytes 6148
  179.3 161.0 %copy-start.247 = (f32[2048]{0:T(1024)S(1)}, f32[2048]{0:T(1024)}, u32[]{:S(2)}) copy-start(f32[2048]{0:T(1024)} %param.36) | copy-start | bytes 24580
  179.3 161.0 %copy-start.248 = (f32[512]{0:T(512)S(1)}, f32[512]{0:T(512)}, u32[]{:S(2)}) copy-start(f32[512]{0:T(512)} %param.34) | copy-start | bytes 6148
  179.3 161.0 %copy-start.249 = (f32[512]{0:T(512)S(1)}, f32[512]{0:T(512)}, u32[]{:S(2)}) copy-start(f32[512]{0:T(512)} %param.38) | copy-start | bytes 6148
  338.8 17.9 %collective-permute-start = (bf16[2048,512]{1,0:T(8,128)(2,1)}, bf16[2048,512]{1,0:T(8,128)(2,1)S(1)}, u32[]{:S(2)}, u32[]{:S(2)}) collective-permute-start(bf16[2048,512]{1,0:T(8,128)(2,1)} %get-tuple-element.535), channel_id=1, source_target_pairs={{0,16},{1,17},{2,18},{3,19},{4,20},{5,21},{6,22},{7,23},{8,24},{9,... | collective-permute-start | bytes 6291464 | tf_op jit(solution)/shard_map/ppermute | solution.py:22
  355.4 30.7 %collective-permute-start.3 = (bf16[2048,512]{1,0:T(8,128)(2,1)}, bf16[2048,512]{1,0:T(8,128)(2,1)}, u32[]{:S(2)}, u32[]{:S(2)}) collective-permute-start(bf16[2048,512]{1,0:T(8,128)(2,1)} %get-tuple-element.204), channel_id=1, source_target_pairs={{16,0},{17,1},{18,2},{19,3},{20,4},{21,5},{22,6},{23,7},{24,8},{25... | collective-permute-start | bytes 6291464 | tf_op jit(solution)/shard_map/ppermute | solution.py:22
  384.2 444.7 %collective-permute-start.1 = (bf16[2048,512]{1,0:T(8,128)(2,1)}, bf16[2048,512]{1,0:T(8,128)(2,1)}, u32[]{:S(2)}, u32[]{:S(2)}) collective-permute-start(bf16[2048,512]{1,0:T(8,128)(2,1)} %get-tuple-element.202), channel_id=1, source_target_pairs={{16,0},{17,1},{18,2},{19,3},{20,4},{21,5},{22,6},{23,7},{24,8},{25... | collective-permute-start | bytes 6291464 | tf_op jit(solution)/shard_map/ppermute | solution.py:22
  386.8 442.1 %copy-start.1 = (bf16[2048,512]{1,0:T(8,128)(2,1)S(1)}, bf16[2048,512]{1,0:T(8,128)(2,1)}, u32[]{:S(2)}) copy-start(bf16[2048,512]{1,0:T(8,128)(2,1)} %copy-done) | copy-start | bytes 6291460
  386.8 442.1 %copy-start.39 = (bf16[512,256]{1,0:T(8,128)(2,1)S(1)}, bf16[512,256]{1,0:T(8,128)(2,1)}, u32[]{:S(2)}) copy-start(bf16[512,256]{1,0:T(8,128)(2,1)} %param.30) | copy-start | bytes 786436
  392.2 44.0 %copy-start.180 = (f32[2048]{0:T(1024)}, f32[2048]{0:T(1024)S(1)}, u32[]{:S(2)}) copy-start(f32[2048]{0:T(1024)S(1)} %broadcast_multiply_fusion.5) | copy-start | bytes 24580 | tf_op jit(solution)/shard_map/cond
  702.5 18.8 %copy-start.161 = (f32[8,64]{0,1:T(8,128)S(1)}, f32[8,64]{0,1:T(8,128)}, u32[]{:S(2)}) copy-start(f32[8,64]{0,1:T(8,128)} %copy-done.160) | copy-start | bytes 6148 | tf_op jit(solution)/shard_map/cond
  702.6 19.4 %copy-start.114 = (f32[8,64]{0,1:T(8,128)S(1)}, f32[8,64]{0,1:T(8,128)}, u32[]{:S(2)}) copy-start(f32[8,64]{0,1:T(8,128)} %copy-done.113) | copy-start | bytes 6148 | tf_op jit(solution)/shard_map/cond
  707.6 20.3 %copy-start.20 = (f32[8,64,64]{2,0,1:T(8,128)S(1)}, f32[8,64,64]{2,0,1:T(8,128)}, u32[]{:S(2)}) copy-start(f32[8,64,64]{2,0,1:T(8,128)} %copy-done.19) | copy-start | bytes 393220 | tf_op jit(solution)/shard_map/cond
  707.7 20.3 %copy-start.110 = (f32[8,64]{1,0:T(8,128)S(1)}, f32[8,64]{1,0:T(8,128)}, u32[]{:S(2)}) copy-start(f32[8,64]{1,0:T(8,128)} %copy-done.109) | copy-start | bytes 6148 | tf_op jit(solution)/shard_map/cond
  710.1 29.0 %copy-start.16 = (f32[8,64,64]{2,0,1:T(8,128)S(1)}, f32[8,64,64]{2,0,1:T(8,128)}, u32[]{:S(2)}) copy-start(f32[8,64,64]{2,0,1:T(8,128)} %copy-done.15) | copy-start | bytes 393220 | tf_op jit(solution)/shard_map/cond
  710.1 29.0 %copy-start.106 = (f32[8,64]{1,0:T(8,128)S(1)}, f32[8,64]{1,0:T(8,128)}, u32[]{:S(2)}) copy-start(f32[8,64]{1,0:T(8,128)} %copy-done.105) | copy-start | bytes 6148 | tf_op jit(solution)/shard_map/cond
  721.3 17.8 %copy-start.183 = (f32[8,64]{1,0:T(8,128)S(1)}, f32[8,64]{1,0:T(8,128)}, u32[]{:S(2)}) copy-start(f32[8,64]{1,0:T(8,128)} %copy-done.182) | copy-start | bytes 6148 | tf_op jit(solution)/shard_map/cond
  722.9 26.3 %copy-start.32 = (f32[64,64,8]{1,2,0:T(8,128)S(1)}, f32[64,64,8]{1,2,0:T(8,128)}, u32[]{:S(2)}) copy-start(f32[64,64,8]{1,2,0:T(8,128)} %copy-done.31) | copy-start | bytes 393220 | tf_op jit(solution)/shard_map/cond
  727.1 22.1 %copy-start.195 = (f32[8,64]{1,0:T(8,128)S(1)}, f32[8,64]{1,0:T(8,128)}, u32[]{:S(2)}) copy-start(f32[8,64]{1,0:T(8,128)} %copy-done.194) | copy-start | bytes 6148 | tf_op jit(solution)/shard_map/cond
  757.6 62.5 %copy-start.76 = (f32[64,512]{1,0:T(8,128)}, f32[64,512]{1,0:T(8,128)S(1)}, u32[]{:S(2)}) copy-start(f32[64,512]{1,0:T(8,128)S(1)} %convolution_multiply_fusion.1) | copy-start | bytes 393220 | tf_op jit(solution)/shard_map/cond
  830.0 48.1 %copy-start.2 = (bf16[2048,512]{1,0:T(8,128)(2,1)}, bf16[2048,512]{1,0:T(8,128)(2,1)S(1)}, u32[]{:S(2)}) copy-start(bf16[2048,512]{1,0:T(8,128)(2,1)S(1)} %get-tuple-element.128) | copy-start | bytes 6291460 | tf_op jit(solution)/shard_map/cond
  1136.4 17.4 %copy-start.163 = (f32[8,64]{0,1:T(8,128)S(1)}, f32[8,64]{0,1:T(8,128)}, u32[]{:S(2)}) copy-start(f32[8,64]{0,1:T(8,128)} %copy-done.162) | copy-start | bytes 6148 | tf_op jit(solution)/shard_map/cond
  1136.4 18.1 %copy-start.116 = (f32[8,64]{0,1:T(8,128)S(1)}, f32[8,64]{0,1:T(8,128)}, u32[]{:S(2)}) copy-start(f32[8,64]{0,1:T(8,128)} %copy-done.115) | copy-start | bytes 6148 | tf_op jit(solution)/shard_map/cond
  1143.3 25.4 %copy-start.18 = (f32[8,64,64]{2,0,1:T(8,128)S(1)}, f32[8,64,64]{2,0,1:T(8,128)}, u32[]{:S(2)}) copy-start(f32[8,64,64]{2,0,1:T(8,128)} %copy-done.17) | copy-start | bytes 393220 | tf_op jit(solution)/shard_map/cond
  1143.3 25.4 %copy-start.108 = (f32[8,64]{1,0:T(8,128)S(1)}, f32[8,64]{1,0:T(8,128)}, u32[]{:S(2)}) copy-start(f32[8,64]{1,0:T(8,128)} %copy-done.107) | copy-start | bytes 6148 | tf_op jit(solution)/shard_map/cond
  1154.9 23.3 %copy-start.34 = (f32[64,64,8]{1,2,0:T(8,128)S(1)}, f32[64,64,8]{1,2,0:T(8,128)}, u32[]{:S(2)}) copy-start(f32[64,64,8]{1,2,0:T(8,128)} %copy-done.33) | copy-start | bytes 393220 | tf_op jit(solution)/shard_map/cond
  1157.5 22.7 %copy-start.197 = (f32[8,64]{1,0:T(8,128)S(1)}, f32[8,64]{1,0:T(8,128)}, u32[]{:S(2)}) copy-start(f32[8,64]{1,0:T(8,128)} %copy-done.196) | copy-start | bytes 6148 | tf_op jit(solution)/shard_map/cond
  (220 other events, 1317.0 us)
Sparse Core Ops, SparseCore 0:
  1298.1 243.7 all-reduce.4
where the time goes:
time: 1580 us; the launch traced here: 1560 us
  local copies, waits for them, and re-layouts  599 us (38%)
  matrix products  348 us (22%)
  other arithmetic  336 us (21%)
  waiting for transfers between devices  188 us (12%)
  blocking collectives  43.9 us (3%)
  loops' own time  24 us (2%)
    psum x1, waiting for transfers between devices, shards(): lax.psum((pieces[0], pieces[1], pieces[2], pieces[3], pieces[4], pieces[5...  188 us
    reshape x8, local copies, waits for them, and re-layouts, attention_parts(): values_near = packed[:, 2 * D:].reshape(block_count, BLK, HEADS, HDIM)  53.9 us
    concatenate x4, local copies, waits for them, and re-layouts, attention_parts(): keys_all = jnp.concatenate([keys_near, keys_far], axis=1)  52.9 us
    concatenate x4, local copies, waits for them, and re-layouts, attention_parts(): values_all = jnp.concatenate([values_near, values_far], axis=1)  52.3 us
    reshape x8, local copies, waits for them, and re-layouts, attention_parts(): keys_near = packed[:, D:2 * D].reshape(block_count, BLK, HEADS, HDIM)  51.6 us
    convert_element_type x8, local copies, waits for them, and re-layouts, attention_parts(): attended = attended.reshape(row_count, D).astype(jnp.bfloat16)  50.6 us
    dot_general x4, matrix products, attention_parts(): jnp.einsum('ithd,ishd->ihts', queries, keys_all, preferred_element_type=j...  50.1 us
    sub x4, other arithmetic, attention_parts(): softmax_out = jax.nn.softmax(scores, axis=-1)  46.4 us
  transfers between devices with their start and end apart: 5, of which 1 were waited for; matrix products, arithmetic and copies ran while one was open for 40% of the time, Pallas kernels for 0%

commit v1 on v0

v1 whole, which is shorter than its diff:
```python
import functools
import math

import jax
import jax.numpy as jnp
from jax import lax
from jax.experimental import pallas as pl
from jax.experimental.pallas import tpu as pltpu
from jax.sharding import PartitionSpec as P

D = 512
HEADS = 8
HDIM = 64
FF = 2048
BLK = 32
SINK = 8
SPAN = 32
T = 2048
NB = T // BLK
TA = 256
TF = 512
FC = 512
GL = 256
GOUT, GQ0, GQ1 = 16384, 18432, 21504
PIECE = 512
GAP = BLK + 1
SCALE = 1.0 / math.sqrt(HDIM)
BF = jnp.bfloat16
F32 = jnp.float32


def dot(a, b):
    return jnp.dot(a, b, preferred_element_type=F32)


def dot_nt(a, b):
    return lax.dot_general(a, b, (((1,), (1,)), ((), ())), preferred_element_type=F32)


def iota(shape, axis):
    return lax.broadcasted_iota(jnp.int32, shape, axis)


def normalise(x):
    xc = x - jnp.mean(x, axis=-1, keepdims=True)
    rstd = lax.rsqrt(jnp.mean(xc * xc, axis=-1, keepdims=True) + 1e-5)
    return xc * rstd, rstd


def normalise_back(g, xhat, rstd, gain):
    gg = g * gain
    return rstd * (
        gg
        - jnp.mean(gg, axis=-1, keepdims=True)
        - xhat * jnp.mean(gg * xhat, axis=-1, keepdims=True)
    )


def spread_heads(x, low, high):
    a, b = x[:, :128], x[:, 128:]
    z = jnp.zeros_like(a)
    rows = ([a * low, z], [a * high, z], [z, b * low], [z, b * high])
    return jnp.concatenate([jnp.concatenate(r, axis=1) for r in rows], axis=0)


def take_heads(x, first):
    r = x.shape[0] // 4
    tiles = [
        jnp.where(first, x[2 * c * r : (2 * c + 1) * r, c * 128 : (c + 1) * 128],
                  x[(2 * c + 1) * r : (2 * c + 2) * r, c * 128 : (c + 1) * 128])
        for c in range(2)
    ]
    return jnp.concatenate(tiles, axis=1)


def spread_even(x, low, high):
    a, b = x[:, :128], x[:, 128:]
    rows = ([a * low, b * low], [a * high, b * high])
    return jnp.concatenate([jnp.concatenate(r, axis=1) for r in rows], axis=0)


def spread_pair(x):
    z = jnp.zeros_like(x[:, :128])
    rows = ([x[:, :128], z], [z, x[:, 128:]])
    return jnp.concatenate([jnp.concatenate(r, axis=1) for r in rows], axis=0)


def beside(ref, count, rows):
    return jnp.concatenate([ref[n * rows : (n + 1) * rows] for n in range(count)], axis=1)


def settle(x):
    y = x.reshape(2, NB, 2 * NB)
    y = y - jnp.max(y, axis=1, keepdims=True)
    ex = jnp.exp(y)
    tot = jnp.sum(ex, axis=1, keepdims=True)
    return (ex * inverse(tot)).reshape(x.shape), (y - jnp.log(tot)).reshape(x.shape)


def settle_back(g, p):
    tot = jnp.sum(g.reshape(2, NB, 2 * NB), axis=1, keepdims=True)
    return g - (p.reshape(2, NB, 2 * NB) * tot).reshape(g.shape)


def wide(acc, rows, lanes=range(D // 128)):
    return jnp.concatenate([acc[c, rows] for c in lanes], axis=1)


def put_wide(acc, rows, value):
    for c in range(value.shape[1] // 128):
        acc[c, rows] = value[:, c * 128 : (c + 1) * 128]


def add_wide(acc, rows, value):
    for c in range(value.shape[1] // 128):
        acc[c, rows] += value[:, c * 128 : (c + 1) * 128]


def block_rows(block):
    return pl.ds(block * GAP, BLK)


def get_blocks(acc, first, count, lanes=range(D // 128)):
    return jnp.concatenate([wide(acc, block_rows(first + n), lanes) for n in range(count)], axis=0)


def put_blocks(acc, first, value, lane=0):
    for n in range(value.shape[0] // BLK):
        for c in range(value.shape[1] // 128):
            part = value[n * BLK : (n + 1) * BLK, c * 128 : (c + 1) * 128]
            acc[lane + c, block_rows(first + n)] = part


def flat_rows(ref, base, step, count):
    parts = [ref[pl.ds(pl.multiple_of(base + c * step, 16), count)] for c in range(D // 128)]
    return jnp.concatenate(parts, axis=1)


def put_flat(ref, base, value):
    rows = value.shape[0]
    for c in range(value.shape[1] // 128):
        ref[pl.ds(pl.multiple_of(base + c * rows, 16), rows)] = value[:, c * 128 : (c + 1) * 128]


def inverse(x):
    r = pl.reciprocal(x, approx=True)
    return r * (2.0 - x * r)


def gelu_both(u):
    c = math.sqrt(2.0 / math.pi)
    e = -2.0 * c / math.log(2.0)
    u2 = u * u
    power = jnp.minimum(u * (e + (e * 0.044715) * u2), 120.0)
    half = pl.reciprocal(1.0 + jnp.exp2(power), approx=True)
    act = u * half
    slope = half + act * (1.0 - half) * (2.0 * c + (6.0 * c * 0.044715) * u2)
    return act, slope


AXES = {16: ((1, 2), (2, 2), (4, 4)), 128: ((1, 4), (32, 4), (4, 8))}


def axes_of(dp):
    if dp in AXES:
        return AXES[dp]
    a = max(n for n in range(1, dp + 1) if dp % (n * n) == 0)
    return (1, a), (a, a), (a * a, dp // (a * a))


class Links:
    def __init__(self, groups):
        self.sec, self.dp = lax.axis_index("section"), lax.axis_index("dp")
        self.levels = []
        for axes in groups:
            own = [lax.rem(lax.div(self.dp, stride), n) for stride, n in axes]
            me, scale = 0, 1
            for (_, n), at in zip(axes, own):
                me, scale = me + at * scale, scale * n
            self.levels.append((axes, own, me))
        self.sizes = [2] + [math.prod(n for _, n in axes) for axes in groups]
        self.first = [0]
        for n in self.sizes:
            self.first.append(self.first[-1] + n - 1)
        self.copies = self.first[-1]

    def place(self, level, k):
        return lax.rem(self.levels[level - 1][2] + k, self.sizes[level])

    def peer(self, level, k):
        if level == 0:
            return (1 - self.sec, self.dp)
        axes, own, _ = self.levels[level - 1]
        place, to = self.place(level, k), self.dp
        for (stride, n), at in zip(axes, own):
            to = to + (lax.rem(place, n) - at) * stride
            place = lax.div(place, n)
        return (self.sec, to)

    def everyone(self):
        return [
            self.peer(level, k)
            for level in range(len(self.sizes))
            for k in range(1, self.sizes[level])
        ]


def all_links(dp):
    a, b, c = axes_of(dp)
    sec = lax.axis_index("section")
    a1 = (a[0] + sec * (b[0] - a[0]), a[1])
    b1 = (b[0] + sec * (a[0] - b[0]), b[1])
    return Links([[a1], [b1], [c]]), Links([[a, b], [c]])


def copies_of(dp):
    a, b, c = axes_of(dp)
    return a[1] * b[1] + c[1] - 1


def remote(src, dst, ssem, rsem, device):
    return pltpu.make_async_remote_copy(
        src_ref=src,
        dst_ref=dst,
        send_sem=ssem,
        recv_sem=rsem,
        device_id=device,
        device_id_type=pl.DeviceIdType.MESH,
    )


class Packet:
    def __init__(self, links, ref, out, base, rows, inboxes, ssem, rsem, osem, number):
        self.links, self.ref, self.out, self.inboxes = links, ref, out, inboxes
        self.ssem, self.rsem, self.osem, self.number = ssem, rsem, osem, number
        self.deep = len(links.sizes)
        self.last = 2 * self.deep
        half = rows // 2
        self.size = [half]
        self.off = [base + links.sec * half]
        self.away = base + (1 - links.sec) * half
        self.inpos = [0, 0 if inboxes[0] is not inboxes[1] else half]
        for level in range(1, self.deep):
            n = links.sizes[level]
            self.size.append(self.size[-1] // n)
            self.off.append(self.off[-1] + links.place(level, 0) * self.size[-1])
            self.inpos.append(self.inpos[-1] + (n - 1) * self.size[-1])

    def rows(self, ref, off, level):
        return ref.at[pl.ds(pl.multiple_of(off, 16), self.size[level])]

    def landing(self, level, k, skip, count):
        box, base = self.inboxes[min(level, 1)]
        at = base + self.inpos[level] + (k - 1) * self.size[level] + skip
        return box, pl.ds(pl.multiple_of(at, 16), count)

    def pieces(self, level):
        count = -(-self.size[level] // PIECE)
        rows = self.size[level] // count
        return [(n * rows, rows) for n in range(count)]

    def reduce_start(self, level, k):
        off = self.away
        if level > 0:
            off = self.off[level - 1] + self.links.place(level, k) * self.size[level]
        for skip, count in self.pieces(level):
            box, rows = self.landing(level, k, skip, count)
            remote(
                self.ref.at[pl.ds(pl.multiple_of(off + skip, 16), count)],
                box.at[rows],
                self.ssem.at[self.number],
                self.rsem.at[self.number, level],
                self.links.peer(level, k),
            ).start()

    def gather_start(self, level, k):
        source = self.ref if level == self.deep - 1 else self.out
        for skip, count in self.pieces(level):
            rows = pl.ds(pl.multiple_of(self.off[level] + skip, 16), count)
            remote(
                source.at[rows],
                self.out.at[rows],
                self.ssem.at[self.number],
                self.rsem.at[self.number, self.deep + level],
                self.links.peer(level, k),
            ).start()

    def arrived(self, level, gathered):
        count = (self.links.sizes[level] - 1) * self.size[level]
        if count == 0:
            return
        if not gathered:
            box, rows = self.landing(level, 1, 0, count)
            what = box.at[rows]
        else:
            base = self.away if level == 0 else self.off[level - 1]
            what = self.out.at[pl.ds(pl.multiple_of(base, 16), count)]
        sem = self.rsem.at[self.number, level + (self.deep if gathered else 0)]
        remote(what, what, self.ssem.at[self.number], sem, self.links.peer(0, 1)).wait_recv()

    def sent(self, source):
        count = 2 * sum((n - 1) * size for n, size in zip(self.links.sizes, self.size))
        what = source.at[pl.ds(0, count)]
        sem = self.rsem.at[self.number, 0]
        remote(what, what, self.ssem.at[self.number], sem, self.links.peer(0, 1)).wait_send()

    def own_copy(self):
        return pltpu.make_async_copy(
            self.rows(self.ref, self.off[-1], -1),
            self.rows(self.out, self.off[-1], -1),
            self.osem.at[self.number],
        )

    def ks(self, level):
        return range(1, self.links.sizes[level])

    def add(self, level):
        size = self.size[level]
        chunk = size // -(-size // 1024)
        wide_sum = self.links.sizes[level] > 2

        @pl.loop(0, size // chunk)
        def _(j):
            rows = pl.ds(pl.multiple_of(self.off[level] + j * chunk, 16), chunk)
            total = self.ref[rows]
            if wide_sum:
                total = total.astype(F32)
            for k in self.ks(level):
                box, came = self.landing(level, k, j * chunk, chunk)
                total += box[came].astype(total.dtype)
            self.ref[rows] = total.astype(BF)

    def step(self, n):
        deep = self.deep
        if 1 <= n <= deep:
            self.arrived(n - 1, False)
            self.add(n - 1)
        if n == deep:
            self.own_copy().start()
        if n == deep + 1:
            self.own_copy().wait()
        if n > deep:
            self.arrived(self.last - n, True)
        if n < deep:
            for k in self.ks(n):
                self.reduce_start(n, k)
        elif n < self.last:
            for k in self.ks(self.last - 1 - n):
                self.gather_start(self.last - 1 - n, k)


PLAN = {
    ("ffnend", 0): (("f0", 0),),
    ("ffn", 1, 2): (("f0", 1),),
    ("ffnend", 1): (("f1", 0),),
    ("ffn", 2, 2): (("f1", 1), ("f0", 2),),
    ("ffnend", 2): (("f2", 0),),
    ("ffn", 3, 1): (("f1", 2),),
    ("ffn", 3, 2): (("f2", 1), ("f0", 3),),
    ("ffnend", 3): (("f1", 3), ("f3", 0),),
    ("six", 3): (("f2", 2),),
    ("six", 4): (("f3", 1),),
    ("six", 6): (("f0", 4),),
    ("sixend",): (("o", 0), ("vf", 0),),
    ("seven", 0, 2): (("f1", 4),),
    ("seven", 0, 3): (("f2", 3), ("o", 1), ("vf", 1),),
    ("seven", 0, 4): (("f3", 2),),
    ("seven", 0, 7): (("f0", 5),),
    ("eight", 0, 0): (("o", 2),),
    ("eight", 0, 1): (("vf", 2),),
    ("eight", 0, 3): (("f3", 3),),
    ("eight", 0, 4): (("f1", 5),),
    ("eight", 0, 6): (("f0", 6),),
    ("nine", 0): (("vf", 3), ("q0", 0),),
    ("seven", 1, 0): (("f2", 4), ("f1", 6),),
    ("seven", 1, 1): (("o", 3),),
    ("seven", 1, 2): (("q0", 1),),
    ("seven", 1, 3): (("f3", 4), ("f0", 7),),
    ("sevenend", 1): (("qa", 0),),
    ("eight", 1, 0): (("f1", 7),),
    ("eight", 1, 1): (("f0", 8),),
    ("eight", 1, 2): (("f2", 5),),
    ("eight", 1, 3): (("q0", 2),),
    ("nine", 1): (("o", 4), ("qv", 0),),
    ("eight", 2, 0): (("qa", 1), ("f1", 8),),
    ("eight", 2, 1): (("f2", 6),),
    ("eight", 2, 2): (("qv", 1), ("f3", 5),),
    ("eight", 2, 3): (("q0", 3),),
    ("nine", 2): (("qk", 0),),
    ("ten",): (("qa", 2), ("o", 5), ("qk", 1), ("z2", 0),),
    ("eleven", 0): (("f2", 7),),
    ("eleven", 1): (("q0", 4),),
    ("eleven", 2): (("qv", 2), ("z2", 1), ("f3", 6),),
    ("eleven", 3): (("qa", 3), ("o", 6), ("f2", 8),),
    ("eleven", 4): (("qk", 2),),
    ("eleven", 6): (("z2", 2),),
    ("eleven", 7): (("q0", 5), ("qv", 3),),
    ("tail",): (
        ("va", 0), ("qa", 4), ("f3", 7), ("qk", 3), ("va", 1), ("o", 7), ("z2", 3), ("q0", 6),
        ("f3", 8), ("qv", 4), ("o", 8), ("va", 2), ("qa", 5), ("qk", 4), ("z2", 4), ("q0", 7),
        ("qa", 6), ("va", 3), ("qv", 5), ("q0", 8), ("qk", 5), ("qv", 6), ("z2", 5), ("qk", 6),
        ("z2", 6),
    ),
}


def kernel(
    dp,
    len_ref,
    tok_ref,
    cot_ref,
    wqkv_ref,
    wout,
    wsort,
    gain_a_ref,
    bias_a_ref,
    gain_f_ref,
    bias_f_ref,
    bias_d_ref,
    wup,
    bup,
    wdown,
    ends_o,
    grads_o,
    sort_o,
    vec_o,
    xs,
    wqkv,
    w1,
    w2,
    cs,
    qs,
    ks,
    vs,
    kts,
    vts,
    kfs,
    vfs,
    ps,
    attt,
    mid,
    nf,
    nft,
    cott,
    acc0,
    acc1,
    mcat,
    mcatt,
    psave,
    summ,
    gm,
    halves,
    actb,
    gpreb,
    gr,
    gz,
    vb,
    vin,
    sem_in,
    ssem,
    rsem,
    out_sem,
    end_send,
    end_recv,
):
    deep, flat = all_links(dp)
    sec = deep.sec
    mine = pl.ds(pl.multiple_of(sec * T, T), T)
    for c in range(4):
        lanes = slice(c * 128, (c + 1) * 128)
        pltpu.make_async_copy(
            tok_ref.at[mine, lanes], xs.at[pl.ds(c * T, T)], sem_in.at[0]
        ).start()
    e0 = len_ref[sec, 0]
    e1 = e0 + len_ref[sec, 1]
    gain_a, bias_a = gain_a_ref[...], bias_a_ref[...]
    gain_f, bias_f = gain_f_ref[...], bias_f_ref[...]
    bias_d = bias_d_ref[...]
    vb[...] = jnp.zeros_like(vb)
    w_copy = pltpu.make_async_copy(wqkv_ref, wqkv, sem_in.at[4])
    w_copy.start()
    x_part = xs.at[pl.ds(0, 4 * T)]
    pltpu.make_async_copy(x_part, x_part, sem_in.at[0]).wait()
    w_copy.wait()
    cot_copy = pltpu.make_async_copy(cot_ref.at[mine], cs, sem_in.at[1])
    cot_copy.start()
    for c in range(FF // FC):
        for l in range(4):
            to = pl.ds((c * 4 + l) * FC, FC)
            lane = l * 128
            pltpu.make_async_copy(
                wup.at[:, pl.ds(c * FC + lane, 128)], w1.at[to], sem_in.at[2]
            ).start()
            pltpu.make_async_copy(
                wdown.at[pl.ds(c * FC, FC), pl.ds(lane, 128)], w2.at[to], sem_in.at[3]
            ).start()

    def packet(number, base, rows, links, box, more=None, ref=gr, out=grads_o):
        boxes = (box, box if more is None else more)
        return Packet(links, ref, out, base, rows, boxes, ssem, rsem, out_sem, number)

    boxes = ((xs, 0), (xs, 4096), (w1, 0), (w2, 0))
    f = [packet(p, p * 4096, 4096, deep, boxes[p]) for p in range(4)]
    parts = dict(f0=f[0], f1=f[1], f2=f[2], f3=f[3])
    if 1024 % (32 * dp) == 0:
        parts["o"] = packet(4, GOUT, 2048, deep, (w1, 4096))
        parts["q0"] = packet(5, GQ0, 3072, deep, (w2, 4096))
        parts["qa"] = packet(6, GQ1, 1024, flat, (w1, 6144))
        parts["qk"] = packet(7, GQ1 + 1024, 1024, flat, (w1, 0))
        parts["qv"] = packet(8, GQ1 + 2048, 1024, flat, (w1, 1024))
        parts["z2"] = packet(9, 0, 1024, flat, (w2, 7168), ref=gz, out=sort_o)
    else:
        parts["qk"] = packet(4, GOUT, 8192, flat, (w1, 0))
        parts["z2"] = packet(5, 0, gz.shape[0], flat, (w2, 4096), ref=gz, out=sort_o)

    class Vectors:
        def __init__(self, number, base):
            self.number, self.rows = number, pl.ds(base, 8)

        def copy(self, level, k):
            at = flat.first[level] + k - 1
            return remote(
                vb.at[self.rows],
                vin.at[at, self.rows],
                ssem.at[self.number],
                rsem.at[self.number, level],
                flat.peer(level, k),
            )

        def step(self, n):
            if n >= 1:
                first, count = flat.first[n - 1], flat.sizes[n - 1] - 1
                if count:
                    came = vin.at[pl.ds(first, count), self.rows]
                    sem = rsem.at[self.number, n - 1]
                    both = remote(came, came, ssem.at[self.number], sem, flat.peer(0, 1))
                    both.wait_send()
                    both.wait_recv()
                for k in range(count):
                    vb[self.rows] += vin[first + k, self.rows]
            if n < len(flat.sizes):
                for k in range(1, flat.sizes[n]):
                    self.copy(n, k).start()

    packets = list(parts.values())
    parts["vf"] = Vectors(10, 0)
    parts["va"] = Vectors(11, 8)
    def steps(*where):
        for name, n in PLAN.get(where, ()):
            if name in parts:
                parts[name].step(n)

    def steps_at(i, *where):
        for place in PLAN:
            if place[:-1] == where:

                @pl.when(i == place[-1])
                def _():
                    steps(*place)

    def end_copies(at, count, far_sec, staged):
        tile = staged.at[pl.ds(pl.multiple_of(at, TA), count)]
        there = ends_o.at[pl.ds(pl.multiple_of(sec * T + at, TA), count)]
        away = remote(tile, there, end_send.at[far_sec], end_recv.at[0], flat.peer(0, 1))
        return away, pltpu.make_async_copy(tile, there, end_send.at[far_sec])

    def put_end(i, far_sec, staged):
        away, here = end_copies(i * TA, TA, far_sec, staged)

        @pl.when(sec == far_sec)
        def _():
            away.start()

        @pl.when(sec != far_sec)
        def _():
            here.start()

    def wait_end(far_sec, staged):
        away, here = end_copies(0, T, far_sec, staged)

        @pl.when(sec == far_sec)
        def _():
            away.wait_send()

        @pl.when(sec != far_sec)
        def _():
            here.wait()

    lane = iota((NB, 128), 1)
    halves[0] = (lane < HDIM).astype(BF)
    halves[1] = (lane >= HDIM).astype(BF)

    @pl.loop(0, T // TA)
    def _(i):
        rows = pl.ds(pl.multiple_of(i * TA, TA), TA)
        xhat, _ = normalise(flat_rows(xs, i * TA, T, TA).astype(F32))
        normed = xhat * gain_a + bias_a
        low = normed.astype(BF)
        packed = dot(low, wqkv[...]).astype(BF)
        qs[rows] = packed[:, :D]
        k, v = packed[:, D : 2 * D], packed[:, 2 * D :]
        ks[rows] = k
        vs[rows] = v
        nb = TA // BLK
        put_blocks(acc0, i * nb, k.astype(F32))
        put_blocks(acc1, i * nb, v.astype(F32))
        summ[pl.ds(pl.multiple_of(i * nb, nb), nb)] = jnp.mean(
            normed.reshape(nb, BLK, D), axis=1
        )

    blk = iota((2 * NB, 2 * NB), 0) & (NB - 1)
    col = iota((2 * NB, 2 * NB), 1) & (NB - 1)
    owner = (blk >= e0).astype(jnp.int32) + (blk >= e1).astype(jnp.int32)
    col_owner = (col >= e0).astype(jnp.int32) + (col >= e1).astype(jnp.int32)
    same = owner == col_owner
    allowed = same & (col <= blk)
    before = same & (col < blk)
    a = iota((HEADS * SPAN, D), 0)
    b = iota((HEADS * SPAN, D), 1)
    gap = jnp.where(a >> 5 == b >> 6, (b & (HDIM - 1)) - (a & (SPAN - 1)), -1000)
    row = iota((NB, D), 0)
    firsts = (jnp.int32(0), e0, e1)
    lasts = (e0, e1, jnp.int32(NB))
    logits = dot(summ[...].astype(BF), wsort[...])
    high = logits.astype(BF)
    rest = logits - high.astype(F32)
    middle = rest.astype(BF)
    three = jnp.concatenate([high, middle, (rest - middle.astype(F32)).astype(BF)], axis=0)
    placed = jnp.zeros((NB, D), F32)
    for s in range(3):
        moved = dot(three, (gap == firsts[s]).astype(BF))
        moved = moved[:NB] + moved[NB : 2 * NB] + moved[2 * NB :]
        placed = jnp.where(row >= firsts[s], moved, placed)
    start = []
    for g in range(2):
        tiles = [placed[:, c : c + 128] for c in (2 * g * 128, (2 * g + 1) * 128)]
        start.append(jnp.where(allowed, jnp.concatenate(tiles, axis=0), -10000.0))

    def sweep(it, cur):
        for n in range(2):
            cur = [x.T for x in cur]
            done = [settle(x) for x in cur]
            for g in range(2):
                psave[2 * it + n, g] = done[g][0]
            cur = [x for _, x in done]
        return tuple(cur)

    lax.fori_loop(0, SINK, sweep, tuple(start))
    for g in range(2):
        mix = jnp.where(before, psave[2 * SINK - 1, g], 0.0)
        mcat[g] = mix.astype(BF)
        for p in range(2):
            tr = mix[p * NB : (p + 1) * NB].T.astype(BF)
            mcatt[g, p * NB : (p + 1) * NB] = jnp.concatenate([tr[:NB], tr[NB:]], axis=1)

    @pl.loop(0, BLK // 4)
    def _(it):
        low, high = halves[0], halves[1]
        jobs, outs = [], []
        for u in range(4):
            t = it * 4 + u
            every = pl.ds(t, NB, stride=GAP)
            for acc, keep in ((acc0, kts), (acc1, vts)):
                x = wide(acc, every).astype(BF)
                keep[pl.ds(pl.multiple_of(t * NB, NB), NB)] = x
                jobs.append((acc, every, x))
        for acc, every, x in jobs:
            for g in range(2):
                far = dot(mcat[g], spread_even(x[:, g * GL : (g + 1) * GL], low, high))
                outs.append((acc, every, g, far))
        for acc, every, g, far in outs:
            acc[2 * g, every] = far[:NB, :128].astype(BF).astype(F32)
            acc[2 * g + 1, every] = far[NB:, 128:].astype(BF).astype(F32)

    pair = 2 * BLK
    srow = iota((2 * pair, GL), 0)
    tcol = iota((2 * pair, GL), 1) & (pair - 1)
    together = (srow & BLK) == (tcol & BLK)
    own_ok = together & (srow < pair) & ((srow & (BLK - 1)) <= (tcol & (BLK - 1)))
    far_ok = together & (srow >= pair)

    cot_copy.wait()

    @pl.loop(0, T // TA)
    def _(i):
        low, high = halves[0], halves[1]
        first = iota((pair, 128), 1) < HDIM
        seen, scores = [], []
        for j in range(TA // pair):
            block = (i * (TA // pair) + j) * 2
            rows = pl.ds(pl.multiple_of(block * BLK, pair), pair)
            kf = get_blocks(acc0, block, 2).astype(BF)
            vf16 = get_blocks(acc1, block, 2).astype(BF)
            kfs[rows] = kf
            vfs[rows] = vf16
            kseen = jnp.concatenate([ks[rows], kf], axis=0)
            seen.append(jnp.concatenate([vs[rows], vf16], axis=0))
            q = qs[rows] * SCALE
            closed = []
            for n in (block, block + 1):
                opening = (n == 0) | (n == e0) | (n == e1)
                closed.append(jnp.where(opening, 0, 1))
            open_far = jnp.where(tcol < BLK, closed[0], closed[1]) == 1
            valid = own_ok | (far_ok & open_far)
            for g in range(2):
                lanes = slice(g * GL, (g + 1) * GL)
                sc = dot_nt(kseen[:, lanes], spread_heads(q[:, lanes], low, high))
                scores.append(jnp.where(valid, sc, -1e9))
        sc = jnp.concatenate(scores, axis=1)
        ex = jnp.exp(sc - jnp.max(sc, axis=0, keepdims=True))
        w16 = (ex * inverse(jnp.sum(ex, axis=0, keepdims=True))).astype(BF)
        ws = [w16[:, c : c + GL] for c in range(0, w16.shape[1], GL)]
        turned = [w.T for w in ws]
        for n, w in enumerate(ws):
            prow = pl.ds(pl.multiple_of((i * (TA // pair) + n // 2) * pair, pair), pair)
            kept = [w[c : c + BLK] + w[c + BLK : c + pair] for c in (0, pair)]
            ps[prow, n % 2 * GL : (n % 2 + 1) * GL] = jnp.concatenate(kept, axis=0)
        products = [
            dot(w, seen[n // 2][:, n % 2 * GL : (n % 2 + 1) * GL]) for n, w in enumerate(turned)
        ]
        made = [take_heads(r, first).astype(BF) for r in products]
        rows = pl.ds(pl.multiple_of(i * TA, TA), TA)
        att = jnp.concatenate(
            [jnp.concatenate(made[n : n + 2], axis=1) for n in range(0, len(made), 2)], axis=0
        )
        for n in range(2):
            at = pl.multiple_of(i * D + n * TA, TA)
            attt[pl.ds(at, TA)] = att[:, n * TA : (n + 1) * TA]
        x = flat_rows(xs, i * TA, T, TA).astype(F32)
        middle = (x + dot(att, wout[...])).astype(BF)
        mid[rows] = middle
        xhat, _ = normalise(middle.astype(F32))
        nf[rows] = (xhat * gain_f + bias_f).astype(BF)

    barrier = pltpu.get_barrier_semaphore()
    everyone = flat.everyone()
    for device in everyone:
        pl.semaphore_signal(
            barrier, inc=1, device_id=device, device_id_type=pl.DeviceIdType.MESH
        )

    @pl.loop(0, T // TF)
    def _(i):
        rows = pl.ds(pl.multiple_of(i * TF, TF), TF)
        nft[rows] = nf[rows].T
        cott[rows] = cs[rows].T
        put_wide(acc0, rows, jnp.zeros((TF, D), F32))
        put_wide(acc1, rows, jnp.zeros((TF, D), F32))

    pltpu.make_async_copy(w1, w1, sem_in.at[2]).wait()
    pltpu.make_async_copy(w2, w2, sem_in.at[3]).wait()
    pl.semaphore_wait(barrier, len(everyone))

    @pl.loop(0, FF // FC)
    def _(c):
        cols = pl.ds(pl.multiple_of(c * FC, FC), FC)
        @pl.loop(0, T // TF)
        def _(i):
            rows = pl.ds(pl.multiple_of(i * TF, TF), TF)
            up = flat_rows(w1, c * 4 * FC, FC, FC)
            down = flat_rows(w2, c * 4 * FC, FC, FC)
            pre = dot(nf[rows], up) + bup[0:1, cols]
            act, slope = gelu_both(pre)
            act = act.astype(BF)
            gact = dot_nt(cs[rows], down)
            gpre = slope * gact
            vb[pl.ds(4 + c, 1)] += jnp.sum(gpre, axis=0, keepdims=True)
            gpre = gpre.astype(BF)
            add_wide(acc0, rows, dot(act, down))
            add_wide(acc1, rows, dot_nt(gpre, up))
            actb[rows] = act
            gpreb[rows] = gpre
            for chunk in range(FF // FC):

                @pl.when(c == chunk)
                def _():
                    steps_at(i, "ffn", chunk)

        gu = dot(beside(nft, T // TF, D), gpreb[...])
        put_flat(gr, c * 4096, gu.astype(BF))
        gd = dot(beside(cott, T // TF, D), actb[...])
        put_flat(gr, c * 4096 + 2048, gd.T.astype(BF))

        steps_at(c, "ffnend")


    @pl.loop(0, T // TA)
    def _(i):
        rows = pl.ds(pl.multiple_of(i * TA, TA), TA)
        mf = mid[rows].astype(F32)
        gpreb[rows] = (mf + wide(acc0, rows) + bias_d).astype(BF)
        put_end(i, 0, gpreb)
        cot = cs[rows].astype(F32)
        gn = wide(acc1, rows)
        xhat, rstd = normalise(mf)
        vb[0:1] += jnp.sum(gn * xhat, axis=0, keepdims=True)
        vb[1:2] += jnp.sum(gn, axis=0, keepdims=True)
        vb[2:3] += jnp.sum(cot, axis=0, keepdims=True)
        nf[rows] = (cot + normalise_back(gn, xhat, rstd, gain_f)).astype(BF)
        steps_at(i, "six")

    x_copy = pltpu.make_async_copy(tok_ref.at[mine], cs, sem_in.at[0])
    x_copy.start()
    for n in range(T // TA):
        tile = [attt[n * D + m * TA : n * D + (m + 1) * TA] for m in range(2)]
        attt[n * D : (n + 1) * D] = jnp.concatenate(tile, axis=1).T
    gout = dot(beside(attt, T // TA, D), nf[...]).astype(BF)
    put_flat(gr, GOUT, gout)
    gm[...] = jnp.zeros_like(gm)
    steps("sixend")
    x_copy.wait()

    for g in range(2):
        lanes = slice(g * GL, (g + 1) * GL)
        base = (GQ0, GQ1)[g]

        @pl.loop(0, T // TA)
        def _(i):
            rows_t = pl.ds(pl.multiple_of(i * TA, TA), TA)
            gat = dot_nt(nf[rows_t], wout[lanes]).astype(BF)
            low, high = halves[0], halves[1]
            first = iota((pair, 128), 1) < HDIM
            block0 = (iota((BLK, GL), 1) & BLK == 0).astype(BF)
            block1 = (iota((BLK, GL), 1) & BLK != 0).astype(BF)
            blocks, spread, gws, w16s = [], [], [], []
            for j in range(TA // pair):
                at = pl.multiple_of((i * (TA // pair) + j) * pair, pair)
                rows = pl.ds(at, pair)
                vseen = jnp.concatenate([vs[rows, lanes], vfs[rows, lanes]], axis=0)
                gad = spread_heads(gat[j * pair : (j + 1) * pair], low, high)
                gws.append(dot_nt(vseen, gad))
                kept = ps[rows, lanes]
                own, far = kept[:BLK], kept[BLK:]
                w16s.append(
                    jnp.concatenate(
                        [own * block0, own * block1, far * block0, far * block1], axis=0
                    )
                )
                blocks.append(rows)
                spread.append(gad)
            w16 = jnp.concatenate(w16s, axis=1)
            gw = jnp.concatenate(gws, axis=1)
            w = w16.astype(F32)
            gs = w * (gw - jnp.sum(gw * w, axis=0, keepdims=True))
            gs = (gs * SCALE).astype(BF)
            gss = [gs[:, c : c + GL] for c in range(0, gs.shape[1], GL)]
            turned = [part.T for part in gss]
            gvs = [dot(w, gad).astype(BF) for w, gad in zip(w16s, spread)]
            gks = [
                dot(part, spread_heads(qs[rows, lanes], low, high)).astype(BF)
                for part, rows in zip(gss, blocks)
            ]
            gqs = []
            for part, rows in zip(turned, blocks):
                kseen = jnp.concatenate([ks[rows, lanes], kfs[rows, lanes]], axis=0)
                gqs.append(dot(part, kseen))
            for j, (rows, gk, gv, gq) in enumerate(zip(blocks, gks, gvs, gqs)):
                block = (i * (TA // pair) + j) * 2
                cott[rows, lanes] = gk[:pair]
                mid[rows, lanes] = gv[:pair]
                put_blocks(acc0, block, gk[pair:].astype(F32), 2 * g)
                put_blocks(acc1, block, gv[pair:].astype(F32), 2 * g)
                nft[rows, lanes] = take_heads(gq, first).astype(BF)
            if g == 0:
                xhat, _ = normalise(cs[rows_t].astype(F32))
                nl = (xhat * gain_a + bias_a).astype(BF)
                attt[pl.ds(pl.multiple_of(i * D, D), D)] = nl.T
            steps_at(i, "seven", g)

        put_flat(gr, base, dot(beside(attt, T // TA, D), nft[:, lanes]).astype(BF))
        steps("sevenend", g)

        keys, values = (acc0, kts, cott, 1), (acc1, vts, mid, 2)
        for turn, both in enumerate(((keys, values),) if g == 0 else ((values,), (keys,))):
            count = 8 // len(both)

            @pl.loop(0, BLK // count)
            def _(it):
                low, high = halves[0], halves[1]
                jobs, outs = [], []
                for u in range(count):
                    t = it * count + u
                    every = pl.ds(t, NB, stride=GAP)
                    trow = pl.ds(pl.multiple_of(t * NB, NB), NB)
                    for acc, near, _, _ in both:
                        x = jnp.concatenate([acc[2 * g, every], acc[2 * g + 1, every]], axis=1)
                        jobs.append((acc, every, x.astype(BF), near[trow, lanes]))
                spread = [spread_even(x, low, high) for _, _, x, _ in jobs]
                nears = [spread_pair(n) for _, _, _, n in jobs]
                gm[g] += dot_nt(
                    jnp.concatenate(spread, axis=1), jnp.concatenate(nears, axis=1)
                )
                for (acc, every, _, _), x in zip(jobs, spread):
                    outs.append((acc, every, dot(mcatt[g], x)))
                for acc, every, back in outs:
                    acc[2 * g, every] = back[:NB, :128]
                    acc[2 * g + 1, every] = back[NB:, 128:]
                steps_at(it, "eight", g + turn)

            @pl.loop(0, T // TA)
            def _(i):
                rows = pl.ds(pl.multiple_of(i * TA, TA), TA)
                for acc, _, part, _ in both:
                    far = get_blocks(acc, i * (TA // BLK), TA // BLK, (2 * g, 2 * g + 1))
                    part[rows, lanes] = (part[rows, lanes].astype(F32) + far).astype(BF)

            nlt = beside(attt, T // TA, D)
            for _, _, part, n in both:
                put_flat(gr, base + n * 1024, dot(nlt, part[:, lanes]).astype(BF))
            steps("nine", g + turn)

    grads = []
    for g in range(2):
        tiles = []
        for p in range(2):
            lanes = slice(p * NB, (p + 1) * NB)
            tiles.append(jnp.concatenate([gm[g, :NB, lanes], gm[g, NB:, lanes]], axis=1))
        grad = jnp.concatenate(tiles, axis=0) * psave[2 * SINK - 1, g]
        grads.append(jnp.where(before, grad, 0.0))

    def sweep_back(n, grads):
        it = SINK - 1 - n
        for m in (1, 0):
            grads = [settle_back(x, psave[2 * it + m, g]).T for g, x in enumerate(grads)]
        return tuple(grads)

    grads = lax.fori_loop(0, SINK, sweep_back, tuple(grads))
    grads = [jnp.where(allowed, x, 0.0) for x in grads]
    grad = jnp.concatenate([x[c : c + NB] for x in grads for c in (0, NB)], axis=1)
    glog = jnp.zeros((NB, HEADS * SPAN), F32)
    for s in range(3):
        mine_rows = (row >= firsts[s]) & (row < lasts[s])
        kept = jnp.where(mine_rows, grad, 0.0).astype(BF)
        glog = glog + dot_nt(kept, (gap == firsts[s]).astype(BF))
    glog = glog.astype(BF)
    if gz.shape[0] > 1024:
        gz[...] = jnp.zeros_like(gz)
    put_flat(gz, 0, dot(summ[...].astype(BF).T, glog).astype(BF))
    steps("ten")
    summ[...] = dot_nt(glog, wsort[...]) * (1.0 / BLK)

    @pl.loop(0, T // TA)
    def _(i):
        rows = pl.ds(pl.multiple_of(i * TA, TA), TA)
        gp = jnp.concatenate([nft[rows], cott[rows], mid[rows]], axis=1)
        nb = TA // BLK
        gs = summ[pl.ds(pl.multiple_of(i * nb, nb), nb)]
        gn = dot_nt(gp, wqkv[...]) + jnp.broadcast_to(
            gs[:, None, :], (nb, BLK, D)
        ).reshape(TA, D)
        xhat, rstd = normalise(cs[rows].astype(F32))
        vb[8:9] += jnp.sum(gn * xhat, axis=0, keepdims=True)
        vb[9:10] += jnp.sum(gn, axis=0, keepdims=True)
        gx = nf[rows].astype(F32) + normalise_back(gn, xhat, rstd, gain_a)
        actb[rows] = gx.astype(BF)
        put_end(i, 1, actb)
        steps_at(i, "eleven")

    steps("tail")
    vec_o[...] = vb[...]
    wait_end(0, gpreb)
    wait_end(1, actb)
    there = ends_o.at[pl.ds(pl.multiple_of((1 - sec) * T, T), T)]
    remote(there, there, end_send.at[0], end_recv.at[0], flat.peer(0, 1)).wait_recv()
    for part in packets:
        part.sent(gr)


VM = pl.BlockSpec(memory_space=pltpu.VMEM)
HB = pl.BlockSpec(memory_space=pl.ANY)
SM = pl.BlockSpec(memory_space=pltpu.SMEM)


def layer(dp, tokens, cotangent, lengths, w_qkv, w_out, w_sort, vectors, w_up, b_up, w_down):
    sds = jax.ShapeDtypeStruct
    big = pltpu.VMEM((T, D), BF)
    copies = copies_of(dp)
    return pl.pallas_call(
        functools.partial(kernel, dp),
        out_shape=(
            sds((2 * T, D), BF),
            sds((6 * 4096, 128), BF),
            sds((max(1024, 32 * dp), 128), BF),
            sds((16, D), F32),
        ),
        in_specs=[SM, HB, HB, HB] + [VM] * 7 + [HB, VM, HB],
        out_specs=(HB, HB, HB, VM),
        scratch_shapes=[
            pltpu.VMEM((8192, 128), BF),
            pltpu.VMEM((D, 3 * D), BF),
            pltpu.VMEM((8192, 128), BF),
            pltpu.VMEM((8192, 128), BF),
            big,
            big,
            big,
            big,
            big,
            big,
            big,
            big,
            big,
            pltpu.VMEM((2 * T, TA), BF),
            big,
            big,
            big,
            big,
            pltpu.VMEM((D // 128, NB * GAP, 128), F32),
            pltpu.VMEM((D // 128, NB * GAP, 128), F32),
            pltpu.VMEM((2, 2 * NB, 2 * NB), BF),
            pltpu.VMEM((2, 2 * NB, 2 * NB), BF),
            pltpu.VMEM((2 * SINK, 2, 2 * NB, 2 * NB), F32),
            pltpu.VMEM((NB, D), F32),
            pltpu.VMEM((2, 2 * NB, 2 * NB), F32),
            pltpu.VMEM((2, NB, 128), BF),
            big,
            big,
            pltpu.VMEM((6 * 4096, 128), BF),
            pltpu.VMEM((max(1024, 32 * dp), 128), BF),
            pltpu.VMEM((16, D), F32),
            pltpu.VMEM((copies, 16, D), F32),
            pltpu.SemaphoreType.DMA((5,)),
            pltpu.SemaphoreType.DMA((12,)),
            pltpu.SemaphoreType.DMA((12, 8)),
            pltpu.SemaphoreType.DMA((10,)),
            pltpu.SemaphoreType.DMA((2,)),
            pltpu.SemaphoreType.DMA((1,)),
        ],
        compiler_params=pltpu.CompilerParams(
            vmem_limit_bytes=64 * 1024 * 1024, collective_id=0, has_side_effects=True
        ),
    )(lengths, tokens, cotangent, w_qkv, w_out, w_sort, *vectors, w_up, b_up, w_down)


def widen_kernel(
    ends_i, grads_i, sort_i, vec_i, ends_o, gup_o, gdown_o, gqkv_o, gout_o, gsort_o, v0_o, v1_o, v2_o, v3_o, v4_o, bup_o,
    ein, gin, zin, est, gst, esem, gsem, zsem, eout, gout,
):
    rows_e = 256
    steps = 2 * T // rows_e

    def e_in(i):
        rows = pl.ds(pl.multiple_of(i * rows_e, rows_e), rows_e)
        return pltpu.make_async_copy(ends_i.at[rows], ein.at[rows], esem.at[i])

    def g_in(p):
        rows = pl.ds(pl.multiple_of(p * 4096, 4096), 4096)
        return pltpu.make_async_copy(grads_i.at[rows], gin.at[rows], gsem.at[p])

    def e_out(i, count=rows_e, skip=0):
        rows = pl.ds(pl.multiple_of(i * rows_e + skip, count), count)
        slot = lax.rem(i, 8)
        part = est.at[slot, pl.ds(skip, count)]
        return pltpu.make_async_copy(part, ends_o.at[0, rows], eout.at[slot])

    jobs = []
    for p in range(4):
        part = pl.ds(p * FC, FC)
        jobs.append((p, gin, p * 4096, 4, gup_o.at[:, part]))
        jobs.append((p, gin, p * 4096 + 2048, 4, gdown_o.at[part]))
    jobs.append((4, gin, GOUT, 4, gout_o))
    for g, base in enumerate((GQ0, GQ1)):
        for n in range(3):
            jobs.append((5, gin, base + n * 1024, 2, gqkv_o.at[:, pl.ds(n * D + g * GL, GL)]))
    jobs.append((6, zin, 0, 2, gsort_o))

    def job_out(n, count=D, skip=0):
        _, _, _, tiles, to = jobs[n]
        rows = pl.ds(skip, count)
        part = gst.at[n % 5, rows, pl.ds(0, tiles * 128)]
        return pltpu.make_async_copy(part, to.at[rows], gout.at[n % 5])

    for i in range(steps):
        e_in(i).start()
    for p in range(6):
        g_in(p).start()
    z_in = pltpu.make_async_copy(sort_i.at[pl.ds(0, 1024)], zin, zsem.at[0])
    z_in.start()
    for n, vec_o in zip((8, 9, 0, 1, 2), (v0_o, v1_o, v2_o, v3_o, v4_o)):
        vec_o[...] = vec_i[n : n + 1]
    for n in range(4):
        bup_o[:, n * D : (n + 1) * D] = vec_i[4 + n : 5 + n]

    @pl.loop(0, steps)
    def _(i):
        @pl.when(i >= 8)
        def _():
            e_out(i - 8).wait()

        e_in(i).wait()
        rows = pl.ds(pl.multiple_of(i * rows_e, rows_e), rows_e)
        est[lax.rem(i, 8)] = ein[rows].astype(F32)
        for n in range(2):
            e_out(i, rows_e // 2, n * (rows_e // 2)).start()

    z_in.wait()
    for n, (p, source, base, tiles, _) in enumerate(jobs):
        if p < 5 and (n == 0 or jobs[n - 1][0] != p):
            g_in(p).wait()
        if n == 8:
            g_in(5).wait()
        if n >= 5:
            job_out(n - 5).wait()
        for c in range(tiles):
            gst[n % 5, :, c * 128 : (c + 1) * 128] = source[
                base + c * 512 : base + (c + 1) * 512
            ].astype(F32)
        for m in range(4):
            job_out(n, D // 4, m * (D // 4)).start()
    for n in range(len(jobs) - 5, len(jobs)):
        job_out(n).wait()
    for i in range(steps - 8, steps):
        e_out(i).wait()


def widen(ends, grads, sort, vec):
    sds = jax.ShapeDtypeStruct
    return pl.pallas_call(
        widen_kernel,
        out_shape=(
            sds((1, 2 * T, D), F32),
            sds((D, FF), F32),
            sds((FF, D), F32),
            sds((D, 3 * D), F32),
            sds((D, D), F32),
            sds((D, HEADS * SPAN), F32),
        )
        + (sds((1, D), F32),) * 5
        + (sds((1, FF), F32),),
        in_specs=[HB] * 3 + [VM],
        out_specs=(HB,) * 6 + (VM,) * 6,
        scratch_shapes=[
            pltpu.VMEM((2 * T, D), BF),
            pltpu.VMEM((6 * 4096, 128), BF),
            pltpu.VMEM((1024, 128), BF),
            pltpu.VMEM((8, 256, D), F32),
            pltpu.VMEM((5, D, D), F32),
            pltpu.SemaphoreType.DMA((16,)),
            pltpu.SemaphoreType.DMA((6,)),
            pltpu.SemaphoreType.DMA((1,)),
            pltpu.SemaphoreType.DMA((8,)),
            pltpu.SemaphoreType.DMA((5,)),
        ],
        compiler_params=pltpu.CompilerParams(vmem_limit_bytes=62 * 1024 * 1024),
    )(ends, grads, sort, vec)


def shards(
    dp,
    tokens,
    lengths,
    w_qkv,
    w_out,
    w_sort,
    gain_attn,
    bias_attn,
    gain_ffn,
    bias_ffn,
    w_up,
    bias_up,
    w_down,
    bias_down,
    cotangent,
):
    vectors = [v[None] for v in (gain_attn, bias_attn, gain_ffn, bias_ffn, bias_down)]
    results = layer(
        dp,
        tokens,
        cotangent,
        lengths,
        w_qkv,
        w_out,
        w_sort,
        vectors,
        w_up,
        bias_up[None],
        w_down,
    )
    ends, gup, gdown, gqkv, gout, gsort, *small = widen(*results)
    g_attn, b_attn, g_ffn, b_ffn, b_down, b_up = (v.reshape(-1) for v in small)
    return (
        ends,
        gqkv,
        gout,
        gsort,
        g_attn,
        b_attn,
        g_ffn,
        b_ffn,
        gup,
        b_up,
        gdown,
        b_down,
    )


def solution(mesh):
    rep = [P()] * 11
    return jax.shard_map(
        functools.partial(shards, mesh.shape["dp"]),
        mesh=mesh,
        in_specs=(P("dp", None), P("dp", None), *rep, P("dp", None)),
        out_specs=(P("section", "dp", None), *rep),
        check_vma=False,
    )
```

time: 1580 us -> 151 us (0.10); the launches traced: 1560 us -> 151 us
  local copies, waits for them, and re-layouts: 599 us -> 0 us
  matrix products: 348 us -> 0 us
  other arithmetic: 336 us -> 0 us
  waiting for transfers between devices: 188 us -> 0 us
  Pallas kernels: 0 us -> 150 us
  blocking collectives: 43.9 us -> 0 us
  loops' own time: 24 us -> 0 us
    dot_general x60 -> x0, matrix products: 348 us -> none  [the longest x4 50.1 us: attention_parts(): jnp.einsum('ithd,ishd->ihts', queries, keys_all, preferred_element_type=j...]
    reshape x35 -> x0, local copies, waits for them, and re-layouts: 191 us -> none  [the longest x8 53.9 us: attention_parts(): values_near = packed[:, 2 * D:].reshape(block_count, BLK, HEADS, HDIM)]
    psum x1 -> x0, waiting for transfers between devices: 188 us -> none  [shards(): lax.psum((pieces[0], pieces[1], pieces[2], pieces[3], pieces[4], pieces[5...]
    pallas_call x0 -> x2, Pallas kernels: none -> 150 us  [the longest x1 137 us: layer(): pl.pallas_call(functools.partial(kernel, dp), out_shape=(sds((2 * T, D),...]
    concatenate x12 -> x0, local copies, waits for them, and re-layouts: 109 us -> none  [the longest x4 52.9 us: attention_parts(): keys_all = jnp.concatenate([keys_near, keys_far], axis=1)]
    convert_element_type x16 -> x0, local copies, waits for them, and re-layouts: 92.3 us -> none  [the longest x8 50.6 us: attention_parts(): attended = attended.reshape(row_count, D).astype(jnp.bfloat16)]
    reduce_sum x114 -> x0, other arithmetic: 81.8 us -> none  [the longest x48 29 us: doubly_stochastic_balance(): current = current - jax.nn.logsumexp(current, axis=2, keepdims=True)]
    concatenate x16 -> x0, other arithmetic: 80.7 us -> none  [the longest x4 33.9 us: attention_parts(): keys_all = jnp.concatenate([keys_near, keys_far], axis=1)]
  transfers between devices with their start and end apart: 5 -> 0, of which waited for: 1 -> 0; matrix products, arithmetic and copies ran while one was open for 40% -> 0% of each run, Pallas kernels for 0% -> 0%
where the time goes in v1:
time: 151 us
  Pallas kernels  150 us (99%)
    pallas_call x1, Pallas kernels, layer(): pl.pallas_call(functools.partial(kernel, dp), out_shape=(sds((2 * T, D),...  137 us
    pallas_call x1, Pallas kernels, widen(): pl.pallas_call(widen_kernel, out_shape=(sds((1, 2 * T, D), F32), sds((D,...  13.1 us

profile of v1, /device:TPU:0, one launch (start us, length us, event | category | flops | bytes accessed | tf_op | source)
XLA Modules:
  0.0 151.2 jit_solution(961511830386252006)
XLA Ops:
  0.6 137.2 %shard_map.229 = (bf16[4096,512]{1,0:T(8,128)(2,1)}, bf16[24576,128]{1,0:T(8,128)(2,1)}, bf16[1024,128]{1,0:T(8,128)(2,1)}, f32[16,512]{1,0:T(8,128)}) custom-call(s32[2,3]{1,0:T(2,128)} %len_ref.1, bf16[4096,512]{1,0:T(8,128)(2,1)} %tok_ref.1, bf16[4096,512]{1,0:T(8,128)(2,1)} %cot_ref.1, bf16[512,1536]{1,0:T(8,128)(2,1)} %wqkv_ref.1, ...), custom_call_target="tpu_custom_call" | custom-call | tf_op jit(solution)/shard_map/pallas_call | solution.py:978
  137.9 13.1 %shard_map.230 = (f32[1,4096,512]{2,1,0:T(8,128)}, f32[512,2048]{1,0:T(8,128)}, f32[2048,512]{1,0:T(8,128)}, f32[512,1536]{1,0:T(8,128)}, f32[512,512]{1,0:T(8,1...) custom-call(bf16[4096,512]{1,0:T(8,128)(2,1)} %get-tuple-element.28., ...), custom_call_target="tpu_custom_call" | custom-call | tf_op jit(solution)/shard_map/pallas_call | solution.py:1117

commit v2 on v1

--- a/solution.py
+++ b/solution.py
@@ -22,6 +22,7 @@
 FC = 512
 GL = 256
 GOUT, GQ0, GQ1 = 16384, 18432, 21504
+ORDER = ((0, 1, 2), (1, 0, 2))
 PIECE = 512
 GAP = BLK + 1
 SCALE = 1.0 / math.sqrt(HDIM)
@@ -351,55 +352,45 @@
 
 PLAN = {
     ("ffnend", 0): (("f0", 0),),
-    ("ffn", 1, 2): (("f0", 1),),
+    ("ffn", 1, 1): (("f0", 1),),
     ("ffnend", 1): (("f1", 0),),
-    ("ffn", 2, 2): (("f1", 1), ("f0", 2),),
+    ("ffn", 2, 0): (("f0", 2),),
+    ("ffn", 2, 1): (("f1", 1),),
+    ("ffn", 2, 3): (("f0", 3),),
     ("ffnend", 2): (("f2", 0),),
-    ("ffn", 3, 1): (("f1", 2),),
-    ("ffn", 3, 2): (("f2", 1), ("f0", 3),),
-    ("ffnend", 3): (("f1", 3), ("f3", 0),),
-    ("six", 3): (("f2", 2),),
-    ("six", 4): (("f3", 1),),
-    ("six", 6): (("f0", 4),),
-    ("sixend",): (("o", 0), ("vf", 0),),
-    ("seven", 0, 2): (("f1", 4),),
-    ("seven", 0, 3): (("f2", 3), ("o", 1), ("vf", 1),),
-    ("seven", 0, 4): (("f3", 2),),
-    ("seven", 0, 7): (("f0", 5),),
+    ("ffn", 3, 0): (("f1", 2),),
+    ("ffn", 3, 1): (("f2", 1),),
+    ("ffn", 3, 3): (("f0", 4), ("f1", 3),),
+    ("ffnend", 3): (("f3", 0),),
+    ("six", 0): (("f2", 2),),
+    ("six", 3): (("f3", 1),),
+    ("six", 7): (("f0", 5),),
+    ("sixend",): (("o", 0),),
+    ("seven", 0, 2): (("f3", 2),),
+    ("seven", 0, 3): (("f1", 4), ("o", 1),),
+    ("seven", 0, 4): (("f2", 3), ("f0", 6),),
+    ("seven", 0, 6): (("f3", 3),),
     ("eight", 0, 0): (("o", 2),),
-    ("eight", 0, 1): (("vf", 2),),
-    ("eight", 0, 3): (("f3", 3),),
-    ("eight", 0, 4): (("f1", 5),),
-    ("eight", 0, 6): (("f0", 6),),
-    ("nine", 0): (("vf", 3), ("q0", 0),),
-    ("seven", 1, 0): (("f2", 4), ("f1", 6),),
-    ("seven", 1, 1): (("o", 3),),
-    ("seven", 1, 2): (("q0", 1),),
-    ("seven", 1, 3): (("f3", 4), ("f0", 7),),
-    ("sevenend", 1): (("qa", 0),),
-    ("eight", 1, 0): (("f1", 7),),
-    ("eight", 1, 1): (("f0", 8),),
-    ("eight", 1, 2): (("f2", 5),),
-    ("eight", 1, 3): (("q0", 2),),
-    ("nine", 1): (("o", 4), ("qv", 0),),
-    ("eight", 2, 0): (("qa", 1), ("f1", 8),),
-    ("eight", 2, 1): (("f2", 6),),
-    ("eight", 2, 2): (("qv", 1), ("f3", 5),),
-    ("eight", 2, 3): (("q0", 3),),
-    ("nine", 2): (("qk", 0),),
-    ("ten",): (("qa", 2), ("o", 5), ("qk", 1), ("z2", 0),),
-    ("eleven", 0): (("f2", 7),),
-    ("eleven", 1): (("q0", 4),),
-    ("eleven", 2): (("qv", 2), ("z2", 1), ("f3", 6),),
-    ("eleven", 3): (("qa", 3), ("o", 6), ("f2", 8),),
-    ("eleven", 4): (("qk", 2),),
-    ("eleven", 6): (("z2", 2),),
-    ("eleven", 7): (("q0", 5), ("qv", 3),),
+    ("nine", 0): (("f1", 5), ("f0", 7), ("q0", 0),),
+    ("seven", 1, 1): (("f2", 4),),
+    ("seven", 1, 2): (("o", 3),),
+    ("seven", 1, 3): (("f0", 8), ("f1", 6),),
+    ("seven", 1, 4): (("q0", 1), ("f3", 4),),
+    ("nine", 1): (("f2", 5), ("f1", 7), ("qv", 0),),
+    ("eight", 2, 0): (("o", 4),),
+    ("eight", 2, 2): (("q0", 2),),
+    ("nine", 2): (("f1", 8), ("qv", 1), ("qk", 0),),
+    ("ten",): (("f2", 6), ("f3", 5), ("q0", 3), ("qk", 1), ("o", 5), ("z2", 0),),
+    ("eleven", 1): (("qv", 2),),
+    ("eleven", 2): (("z2", 1),),
+    ("eleven", 4): (("f2", 7),),
+    ("eleven", 5): (("q0", 4), ("f3", 6),),
+    ("eleven", 6): (("qv", 3),),
+    ("eleven", 7): (("f2", 8), ("qk", 2), ("o", 6),),
     ("tail",): (
-        ("va", 0), ("qa", 4), ("f3", 7), ("qk", 3), ("va", 1), ("o", 7), ("z2", 3), ("q0", 6),
-        ("f3", 8), ("qv", 4), ("o", 8), ("va", 2), ("qa", 5), ("qk", 4), ("z2", 4), ("q0", 7),
-        ("qa", 6), ("va", 3), ("qv", 5), ("q0", 8), ("qk", 5), ("qv", 6), ("z2", 5), ("qk", 6),
-        ("z2", 6),
+        ("va", 0), ("z2", 2), ("va", 1), ("q0", 5), ("f3", 7), ("qv", 4), ("qk", 3), ("o", 7),
+        ("z2", 3), ("va", 2), ("f3", 8), ("q0", 6), ("o", 8), ("qk", 4), ("va", 3), ("z2", 4),
+        ("qv", 5), ("q0", 7), ("qv", 6), ("qk", 5), ("q0", 8), ("z2", 5), ("qk", 6), ("z2", 6),
     ),
 }
 
@@ -505,17 +496,16 @@
     if 1024 % (32 * dp) == 0:
         parts["o"] = packet(4, GOUT, 2048, deep, (w1, 4096))
         parts["q0"] = packet(5, GQ0, 3072, deep, (w2, 4096))
-        parts["qa"] = packet(6, GQ1, 1024, flat, (w1, 6144))
-        parts["qk"] = packet(7, GQ1 + 1024, 1024, flat, (w1, 0))
-        parts["qv"] = packet(8, GQ1 + 2048, 1024, flat, (w1, 1024))
+        parts["qk"] = packet(6, GQ1, 1024, flat, (w1, 0))
+        parts["qv"] = packet(7, GQ1 + 1024, 2048, flat, (w1, 6144))
         parts["z2"] = packet(9, 0, 1024, flat, (w2, 7168), ref=gz, out=sort_o)
     else:
         parts["qk"] = packet(4, GOUT, 8192, flat, (w1, 0))
         parts["z2"] = packet(5, 0, gz.shape[0], flat, (w2, 4096), ref=gz, out=sort_o)
 
     class Vectors:
-        def __init__(self, number, base):
-            self.number, self.rows = number, pl.ds(base, 8)
+        def __init__(self, number, base, count):
+            self.number, self.rows = number, pl.ds(base, count)
 
         def copy(self, level, k):
             at = flat.first[level] + k - 1
@@ -543,8 +533,7 @@
                     self.copy(n, k).start()
 
     packets = list(parts.values())
-    parts["vf"] = Vectors(10, 0)
-    parts["va"] = Vectors(11, 8)
+    parts["va"] = Vectors(10, 0, 16)
     def steps(*where):
         for name, n in PLAN.get(where, ()):
             if name in parts:
@@ -867,7 +856,8 @@
                 attt[pl.ds(pl.multiple_of(i * D, D), D)] = nl.T
             steps_at(i, "seven", g)
 
-        put_flat(gr, base, dot(beside(attt, T // TA, D), nft[:, lanes]).astype(BF))
+        gq = dot(beside(attt, T // TA, D), nft[:, lanes]).astype(BF)
+        put_flat(gr, base + ORDER[g].index(0) * 1024, gq)
         steps("sevenend", g)
 
         keys, values = (acc0, kts, cott, 1), (acc1, vts, mid, 2)
@@ -906,7 +896,8 @@
 
             nlt = beside(attt, T // TA, D)
             for _, _, part, n in both:
-                put_flat(gr, base + n * 1024, dot(nlt, part[:, lanes]).astype(BF))
+                at = base + ORDER[g].index(n) * 1024
+                put_flat(gr, at, dot(nlt, part[:, lanes]).astype(BF))
             steps("nine", g + turn)
 
     grads = []
@@ -1059,8 +1050,8 @@
         jobs.append((p, gin, p * 4096 + 2048, 4, gdown_o.at[part]))
     jobs.append((4, gin, GOUT, 4, gout_o))
     for g, base in enumerate((GQ0, GQ1)):
-        for n in range(3):
-            jobs.append((5, gin, base + n * 1024, 2, gqkv_o.at[:, pl.ds(n * D + g * GL, GL)]))
+        for at, n in enumerate(ORDER[g]):
+            jobs.append((5, gin, base + at * 1024, 2, gqkv_o.at[:, pl.ds(n * D + g * GL, GL)]))
     jobs.append((6, zin, 0, 2, gsort_o))
 
     def job_out(n, count=D, skip=0):

time: 151 us -> 153 us (1.013)
  Pallas kernels: 150 us -> 152 us
where the time goes in v2:
time: 153 us; the launch traced here: 152 us
  Pallas kernels  152 us (99%)
    pallas_call x1, Pallas kernels, layer(): pl.pallas_call(functools.partial(kernel, dp), out_shape=(sds((2 * T, D),...  138 us
    pallas_call x1, Pallas kernels, widen(): pl.pallas_call(widen_kernel, out_shape=(sds((1, 2 * T, D), F32), sds((D,...  13.1 us

profile of v2, /device:TPU:0, one launch (start us, length us, event | category | flops | bytes accessed | tf_op | source)
XLA Modules:
  0.0 152.4 jit_solution(11001373333994513476)
XLA Ops:
  0.6 138.4 %shard_map.229 = (bf16[4096,512]{1,0:T(8,128)(2,1)}, bf16[24576,128]{1,0:T(8,128)(2,1)}, bf16[1024,128]{1,0:T(8,128)(2,1)}, f32[16,512]{1,0:T(8,128)}) custom-call(s32[2,3]{1,0:T(2,128)} %len_ref.1, bf16[4096,512]{1,0:T(8,128)(2,1)} %tok_ref.1, bf16[4096,512]{1,0:T(8,128)(2,1)} %cot_ref.1, bf16[512,1536]{1,0:T(8,128)(2,1)} %wqkv_ref.1, ...), custom_call_target="tpu_custom_call" | custom-call | tf_op jit(solution)/shard_map/pallas_call | solution.py:969
  139.1 13.1 %shard_map.230 = (f32[1,4096,512]{2,1,0:T(8,128)}, f32[512,2048]{1,0:T(8,128)}, f32[2048,512]{1,0:T(8,128)}, f32[512,1536]{1,0:T(8,128)}, f32[512,512]{1,0:T(8,1...) custom-call(bf16[4096,512]{1,0:T(8,128)(2,1)} %get-tuple-element.28., ...), custom_call_target="tpu_custom_call" | custom-call | tf_op jit(solution)/shard_map/pallas_call | solution.py:1108

commit v3 on v2

--- a/solution.py
+++ b/solution.py
@@ -352,45 +352,47 @@
 
 PLAN = {
     ("ffnend", 0): (("f0", 0),),
-    ("ffn", 1, 1): (("f0", 1),),
+    ("ffn", 1, 2): (("f0", 1),),
     ("ffnend", 1): (("f1", 0),),
-    ("ffn", 2, 0): (("f0", 2),),
-    ("ffn", 2, 1): (("f1", 1),),
-    ("ffn", 2, 3): (("f0", 3),),
+    ("ffn", 2, 2): (("f1", 1), ("f0", 2),),
     ("ffnend", 2): (("f2", 0),),
-    ("ffn", 3, 0): (("f1", 2),),
-    ("ffn", 3, 1): (("f2", 1),),
-    ("ffn", 3, 3): (("f0", 4), ("f1", 3),),
-    ("ffnend", 3): (("f3", 0),),
-    ("six", 0): (("f2", 2),),
-    ("six", 3): (("f3", 1),),
-    ("six", 7): (("f0", 5),),
+    ("ffn", 3, 1): (("f1", 2),),
+    ("ffn", 3, 2): (("f2", 1), ("f0", 3),),
+    ("ffnend", 3): (("f1", 3), ("f3", 0),),
+    ("six", 3): (("f2", 2),),
+    ("six", 4): (("f3", 1),),
+    ("six", 6): (("f0", 4),),
     ("sixend",): (("o", 0),),
-    ("seven", 0, 2): (("f3", 2),),
-    ("seven", 0, 3): (("f1", 4), ("o", 1),),
-    ("seven", 0, 4): (("f2", 3), ("f0", 6),),
-    ("seven", 0, 6): (("f3", 3),),
-    ("eight", 0, 0): (("o", 2),),
-    ("nine", 0): (("f1", 5), ("f0", 7), ("q0", 0),),
-    ("seven", 1, 1): (("f2", 4),),
-    ("seven", 1, 2): (("o", 3),),
-    ("seven", 1, 3): (("f0", 8), ("f1", 6),),
-    ("seven", 1, 4): (("q0", 1), ("f3", 4),),
-    ("nine", 1): (("f2", 5), ("f1", 7), ("qv", 0),),
-    ("eight", 2, 0): (("o", 4),),
-    ("eight", 2, 2): (("q0", 2),),
-    ("nine", 2): (("f1", 8), ("qv", 1), ("qk", 0),),
-    ("ten",): (("f2", 6), ("f3", 5), ("q0", 3), ("qk", 1), ("o", 5), ("z2", 0),),
-    ("eleven", 1): (("qv", 2),),
-    ("eleven", 2): (("z2", 1),),
-    ("eleven", 4): (("f2", 7),),
-    ("eleven", 5): (("q0", 4), ("f3", 6),),
-    ("eleven", 6): (("qv", 3),),
-    ("eleven", 7): (("f2", 8), ("qk", 2), ("o", 6),),
+    ("seven", 0, 3): (("f1", 4),),
+    ("seven", 0, 4): (("f2", 3), ("o", 1),),
+    ("seven", 0, 5): (("f3", 2),),
+    ("eight", 0, 0): (("f0", 5),),
+    ("eight", 0, 3): (("o", 2),),
+    ("nine", 0): (("f3", 3), ("f1", 5), ("q0", 0),),
+    ("seven", 1, 0): (("f0", 6),),
+    ("seven", 1, 2): (("f2", 4),),
+    ("seven", 1, 3): (("o", 3), ("q0", 1),),
+    ("seven", 1, 4): (("f1", 6),),
+    ("eight", 1, 0): (("f3", 4),),
+    ("eight", 1, 1): (("f0", 7),),
+    ("nine", 1): (("qv", 0),),
+    ("eight", 2, 0): (("q0", 2),),
+    ("eight", 2, 1): (("f2", 5),),
+    ("eight", 2, 2): (("f0", 8),),
+    ("eight", 2, 3): (("o", 4),),
+    ("nine", 2): (("qv", 1), ("f1", 7), ("qk", 0),),
+    ("ten",): (("q0", 3), ("f3", 5), ("f2", 6), ("z2", 0),),
+    ("eleven", 0): (("f1", 8), ("qk", 1), ("o", 5),),
+    ("eleven", 1): (("qv", 2), ("z2", 1),),
+    ("eleven", 2): (("f3", 6),),
+    ("eleven", 3): (("q0", 4),),
+    ("eleven", 5): (("f2", 7),),
+    ("eleven", 7): (("qv", 3),),
     ("tail",): (
-        ("va", 0), ("z2", 2), ("va", 1), ("q0", 5), ("f3", 7), ("qv", 4), ("qk", 3), ("o", 7),
-        ("z2", 3), ("va", 2), ("f3", 8), ("q0", 6), ("o", 8), ("qk", 4), ("va", 3), ("z2", 4),
-        ("qv", 5), ("q0", 7), ("qv", 6), ("qk", 5), ("q0", 8), ("z2", 5), ("qk", 6), ("z2", 6),
+        ("va", 0), ("o", 6), ("qk", 2), ("f2", 8), ("va", 1), ("z2", 2), ("q0", 5), ("f3", 7),
+        ("qv", 4), ("qk", 3), ("o", 7), ("va", 2), ("z2", 3), ("q0", 6), ("f3", 8), ("o", 8),
+        ("qk", 4), ("va", 3), ("qv", 5), ("z2", 4), ("q0", 7), ("qv", 6), ("qk", 5), ("q0", 8),
+        ("z2", 5), ("qk", 6), ("z2", 6),
     ),
 }
 

time: 153 us -> 151 us (0.987)
  Pallas kernels: 152 us -> 149 us
    pallas_call x1, Pallas kernels: 138 us -> 136 us  [layer(): pl.pallas_call(functools.partial(kernel, dp), out_shape=(sds((2 * T, D),...]
where the time goes in v3:
time: 151 us; the launch traced here: 150 us
  Pallas kernels  149 us (99%)
    pallas_call x1, Pallas kernels, layer(): pl.pallas_call(functools.partial(kernel, dp), out_shape=(sds((2 * T, D),...  136 us
    pallas_call x1, Pallas kernels, widen(): pl.pallas_call(widen_kernel, out_shape=(sds((1, 2 * T, D), F32), sds((D,...  13.1 us

profile of v3, /device:TPU:0, one launch (start us, length us, event | category | flops | bytes accessed | tf_op | source)
XLA Modules:
  0.0 150.3 jit_solution(10785608169366248336)
XLA Ops:
  0.6 136.3 %shard_map.229 = (bf16[4096,512]{1,0:T(8,128)(2,1)}, bf16[24576,128]{1,0:T(8,128)(2,1)}, bf16[1024,128]{1,0:T(8,128)(2,1)}, f32[16,512]{1,0:T(8,128)}) custom-call(s32[2,3]{1,0:T(2,128)} %len_ref.1, bf16[4096,512]{1,0:T(8,128)(2,1)} %tok_ref.1, bf16[4096,512]{1,0:T(8,128)(2,1)} %cot_ref.1, bf16[512,1536]{1,0:T(8,128)(2,1)} %wqkv_ref.1, ...), custom_call_target="tpu_custom_call" | custom-call | tf_op jit(solution)/shard_map/pallas_call | solution.py:971
  137.0 13.1 %shard_map.230 = (f32[1,4096,512]{2,1,0:T(8,128)}, f32[512,2048]{1,0:T(8,128)}, f32[2048,512]{1,0:T(8,128)}, f32[512,1536]{1,0:T(8,128)}, f32[512,512]{1,0:T(8,1...) custom-call(bf16[4096,512]{1,0:T(8,128)(2,1)} %get-tuple-element.28., ...), custom_call_target="tpu_custom_call" | custom-call | tf_op jit(solution)/shard_map/pallas_call | solution.py:1110
